TPU v7x, 128 devices: a whole 4x4x4 slice. The times are simulated.
128 devices in a mesh: lat: 8 (over x, core), lon: 16 (over z, y).
Axes of the slice: x: 4, y: 4, z: 4, core: 2. Of those that a mesh axis runs over, the one named last changes fastest.
Arguments:
- node_latents: bfloat16 [32768, 512], P(('lat', 'lon')), may hold values from -6 to 6
- edge_latents: bfloat16 [262144, 512], P(('lat', 'lon')), may hold values from -6 to 6
- edge_count: int32 [128], P(('lat', 'lon')), may hold values from 256 to 2048, as said below
- receiver: int32 [262144], P(('lat', 'lon')), may hold values from 0 to 255, as said below
- sender: int32 [262144], P(('lat', 'lon')), may hold values from 0 to 639, as said below
- halo_send: int32 [128, 4, 32], P(('lat', 'lon')), may hold values from 0 to 255
- far_send: int32 [128, 128, 2], P(('lat', 'lon')), may hold values from 0 to 255
- edge_weight_in: bfloat16 [1536, 512], replicated, may hold values from -0.15625 to 0.15625
- edge_bias: float32 [512], replicated, may hold values from -3 to 3
- edge_weight_out: bfloat16 [512, 512], replicated, may hold values from -0.25 to 0.25
- edge_gain: float32 [512], replicated, may hold values from 0.25 to 1.75
- node_weight_in: bfloat16 [1024, 512], replicated, may hold values from -0.1875 to 0.1875
- node_bias: float32 [512], replicated, may hold values from -3 to 3
- node_weight_out: bfloat16 [512, 512], replicated, may hold values from -0.25 to 0.25
- node_gain: float32 [512], replicated, may hold values from 0.25 to 1.75
- cot_nodes: bfloat16 [32768, 512], P(('lat', 'lon')), may hold values from -6 to 6
- cot_edges: bfloat16 [262144, 512], P(('lat', 'lon')), may hold values from -6 to 6
Outputs:
- node_out: bfloat16 [32768, 512], P(('lat', 'lon'))
- edge_out: bfloat16 [262144, 512], P(('lat', 'lon'))
- grad_nodes: bfloat16 [32768, 512], P(('lat', 'lon'))
- grad_edges: bfloat16 [262144, 512], P(('lat', 'lon'))
- grad_edge_weight_in: float32 [1536, 512], replicated
- grad_edge_bias: float32 [512], replicated
- grad_edge_weight_out: float32 [512, 512], replicated
- grad_edge_gain: float32 [512], replicated
- grad_node_weight_in: float32 [1024, 512], replicated
- grad_node_bias: float32 [512], replicated
- grad_node_weight_out: float32 [512, 512], replicated
- grad_node_gain: float32 [512], replicated
Inputs may be any that keep to these rules, and one draw needn't show every extreme that they name: `edge_count`: edge slots of a device past its count are padding; some device has all 2048 slots live in every draw. `receiver`: nondecreasing within each device's 2048 edge slots. `sender`: rows below 256 are the device's own nodes, the next 128 the four neighbours' halo rows, the rest the 2 rows from each peer in device order; halo rows from a band that does not exist are never named.
All inputs are finite; a program needn't handle non-finite values.
Results may differ from a plain program's by a relative error of at most 0.017.
Values may be sent and summed in bfloat16 or wider, within the bound.
A program may use at most 128 MiB of HBM per device.

v0:
```python
from functools import partial

import jax
import jax.numpy as jnp
from jax import lax
from jax.sharding import PartitionSpec as P

EPSILON = 1e-05


def padded(array, sides, width, wrap):
    for axis, dim in sides:
        size, length = (lax.axis_size(axis), array.shape[dim])
        up = [(i, (i + 1) % size) for i in range(size if wrap else size - 1)]
        down = [(j, i) for i, j in up]
        last = lax.slice_in_dim(array, length - width, length, axis=dim)
        first = lax.slice_in_dim(array, 0, width, axis=dim)
        before = lax.ppermute(last, axis, up)
        after = lax.ppermute(first, axis, down)
        array = jnp.concatenate([before, array, after], axis=dim)
    return array


def layer_norm(values, gain_out):
    row_mean = jnp.mean(values, axis=-1, keepdims=True)
    centered = values - row_mean
    variance = jnp.mean(centered * centered, axis=-1, keepdims=True)
    return centered * lax.rsqrt(variance + EPSILON) * gain_out


def edge_update(params, edge_rows, sender_rows, receiver_rows, live_mask):
    weight_in, bias_in, weight_out, gain_out = params
    joined = jnp.concatenate([edge_rows, sender_rows, receiver_rows], axis=1)
    first_layer = jnp.dot(joined, weight_in, preferred_element_type=jnp.float32) + bias_in
    active = jax.nn.silu(first_layer).astype(jnp.bfloat16)
    second = jnp.dot(active, weight_out, preferred_element_type=jnp.float32)
    message = layer_norm(second, gain_out) * live_mask[:, None]
    updated = (edge_rows.astype(jnp.float32) + message).astype(jnp.bfloat16)
    return (updated, message)


def node_update(params, node_rows, gathered):
    weight_in, bias_in, weight_out, gain_out = params
    joined = jnp.concatenate([node_rows, gathered], axis=1)
    first_layer = jnp.dot(joined, weight_in, preferred_element_type=jnp.float32) + bias_in
    active = jax.nn.silu(first_layer).astype(jnp.bfloat16)
    second = jnp.dot(active, weight_out, preferred_element_type=jnp.float32)
    return (node_rows.astype(jnp.float32) + layer_norm(second, gain_out)).astype(jnp.bfloat16)


def shards(
    node_latents,
    edge_latents,
    edge_count,
    receiver,
    sender,
    halo_send,
    far_send,
    edge_weight_in,
    edge_bias,
    edge_weight_out,
    edge_gain,
    node_weight_in,
    node_bias,
    node_weight_out,
    node_gain,
    cot_nodes,
    cot_edges,
):
    node_rows, feature_width = node_latents.shape
    edge_rows = edge_latents.shape[0]
    border = halo_send.shape[2]
    peer_count = far_send.shape[1]
    capacity = far_send.shape[2]
    rim_lists = halo_send[0]
    far_lists = far_send[0].reshape(-1)
    lat_outgoing = jnp.concatenate([node_latents[rim_lists[0]], node_latents[rim_lists[1]]], axis=0)
    lat_rims = padded(lat_outgoing, (("lat", 0),), border, False)
    lon_outgoing = jnp.concatenate([node_latents[rim_lists[2]], node_latents[rim_lists[3]]], axis=0)
    lon_rims = padded(lon_outgoing, (("lon", 0),), border, True)
    far_outgoing = node_latents[far_lists].reshape(peer_count, capacity, feature_width)
    incoming = lax.all_to_all(far_outgoing, ("lat", "lon"), split_axis=0, concat_axis=0, tiled=True)
    sender_table = jnp.concatenate(
        [
            node_latents,
            lat_rims[:border],
            lat_rims[3 * border :],
            lon_rims[:border],
            lon_rims[3 * border :],
            incoming.reshape(peer_count * capacity, feature_width),
        ],
        axis=0,
    )
    live_mask = (lax.iota(jnp.int32, edge_rows) < edge_count[0]).astype(jnp.float32)
    sent_rows = sender_table[sender]
    received_rows = node_latents[receiver]
    edge_params = (edge_weight_in, edge_bias, edge_weight_out, edge_gain)
    node_params = (node_weight_in, node_bias, node_weight_out, node_gain)
    (new_edges, message), edge_back = jax.vjp(
        partial(edge_update, live_mask=live_mask),
        edge_params,
        edge_latents,
        sent_rows,
        received_rows,
    )
    gathered = jax.ops.segment_sum(message, receiver, node_rows, indices_are_sorted=True).astype(
        jnp.bfloat16
    )
    new_nodes, node_back = jax.vjp(node_update, node_params, node_latents, gathered)
    node_grads, from_node, from_gathered = node_back(cot_nodes)
    edge_grads, edge_grad, from_send, from_receive = edge_back(
        (cot_edges, from_gathered.astype(jnp.float32)[receiver])
    )
    totals = from_node.astype(jnp.float32) + jax.ops.segment_sum(
        from_receive.astype(jnp.float32), receiver, node_rows, indices_are_sorted=True
    )
    slot_grads = jax.ops.segment_sum(
        from_send.astype(jnp.float32), sender, node_rows + 4 * border + peer_count * capacity
    )
    totals = totals + slot_grads[:node_rows]
    lat_back = padded(
        slot_grads[node_rows : node_rows + 2 * border].astype(jnp.bfloat16),
        (("lat", 0),),
        border,
        False,
    ).astype(jnp.float32)
    lon_back = padded(
        slot_grads[node_rows + 2 * border : node_rows + 4 * border].astype(jnp.bfloat16),
        (("lon", 0),),
        border,
        True,
    ).astype(jnp.float32)
    totals = (
        totals.at[rim_lists[0]].add(lat_back[:border]).at[rim_lists[1]].add(lat_back[3 * border :])
    )
    totals = (
        totals.at[rim_lists[2]].add(lon_back[:border]).at[rim_lists[3]].add(lon_back[3 * border :])
    )
    far_back = slot_grads[node_rows + 4 * border :].reshape(peer_count, capacity, feature_width)
    returned = lax.all_to_all(
        far_back.astype(jnp.bfloat16), ("lat", "lon"), split_axis=0, concat_axis=0, tiled=True
    ).astype(far_back.dtype)
    totals = totals.at[far_lists].add(returned.reshape(peer_count * capacity, feature_width))
    grad_nodes = totals.astype(jnp.bfloat16)
    every_grad = tuple((grad.astype(jnp.float32) for grad in tuple(edge_grads) + tuple(node_grads)))
    summed = lax.psum(every_grad, ("lat", "lon"))
    return (
        new_nodes,
        new_edges,
        grad_nodes,
        edge_grad,
        summed[0],
        summed[1],
        summed[2],
        summed[3],
        summed[4],
        summed[5],
        summed[6],
        summed[7],
    )


def solution(mesh):
    return jax.shard_map(
        shards,
        mesh=mesh,
        in_specs=(
            P(("lat", "lon"), None),
            P(("lat", "lon"), None),
            P(("lat", "lon")),
            P(("lat", "lon")),
            P(("lat", "lon")),
            P(("lat", "lon"), None, None),
            P(("lat", "lon"), None, None),
            P(),
            P(),
            P(),
            P(),
            P(),
            P(),
            P(),
            P(),
            P(("lat", "lon"), None),
            P(("lat", "lon"), None),
        ),
        out_specs=(
            P(("lat", "lon"), None),
            P(("lat", "lon"), None),
            P(("lat", "lon"), None),
            P(("lat", "lon"), None),
            P(),
            P(),
            P(),
            P(),
            P(),
            P(),
            P(),
            P(),
        ),
        check_vma=False,
    )
```

profile of v0, /device:TPU:1, one launch (start us, length us, event | category | flops | bytes accessed | tf_op | source)
XLA Modules:
  0.0 329.4 jit_solution(7847369240195702064)
XLA Ops:
  8.1 1.6 gather_fusion
  9.7 4.5 %collective-permute-start = (bf16[32,512]{1,0:T(8,128)(2,1)S(1)}, bf16[32,512]{1,0:T(8,128)(2,1)S(1)}, u32[]{:S(2)}, u32[]{:S(2)}) collective-permute-start(bf16[32,512]{1,0:T(8,128)(2,1)S(1)} %gather_fusion), channel_id=1, source_target_pairs={{0,16},{16,32},{32,48},{48,64},{64,80},{80,96},{96,112},{1,17},{17... | collective-permute-start | bytes 98312 | tf_op jit(solution)/shard_map/ppermute | solution.py:18
  14.2 1.6 gather_fusion.1
  15.9 1.9 collective-permute-start.1
  17.8 1.6 gather_fusion.2
  19.4 1.4 collective-permute-start.2
  20.8 1.6 gather_fusion.3
  22.4 5.0 %collective-permute-start.3 = (bf16[32,512]{1,0:T(8,128)(2,1)S(1)}, bf16[32,512]{1,0:T(8,128)(2,1)S(1)}, u32[]{:S(2)}, u32[]{:S(2)}) collective-permute-start(bf16[32,512]{1,0:T(8,128)(2,1)S(1)} %gather_fusion.3), channel_id=1, source_target_pairs={{1,0},{2,1},{3,2},{4,3},{5,4},{6,5},{7,6},{8,7},{9,8},{10,9},{11,1... | collective-permute-start | bytes 98312 | tf_op jit(solution)/shard_map/ppermute | solution.py:19
  28.4 2.2 gather_fusion.4
  31.4 6.4 %all-to-all-start = ((bf16[128,2,512]{2,1,0:T(2,128)(2,1)}), bf16[128,2,512]{2,1,0:T(2,128)(2,1)S(1)}, u32[]{:S(2)}, u32[]{:S(2)}) async-start(bf16[128,2,512]{2,1,0:T(2,128)(2,1)} %reshape.255), calls=%async_computation | async-start | bytes 524288 | tf_op jit(solution)/shard_map/all_to_all | solution.py:82
  38.1 3.1 constant_dynamic-update-slice_fusion.8
  41.9 3.9 %copy.35 = bf16[2048,512]{0,1:T(8,128)(2,1)} copy(bf16[2048,512]{1,0:T(8,128)(2,1)} %param.18) | data formatting | bytes 4194304 | tf_op args[1]
  45.8 9.2 %gather_fusion.6 = bf16[2048,512]{1,0:T(8,128)(2,1)} fusion(bf16[256,512]{1,0:T(8,128)(2,1)S(1)} %copy-done.1, s32[2048]{0:T(1024)S(1)} %fusion.63), kind=kCustom, calls=%fused_computation.6 | custom fusion | bytes 4202496 | tf_op jit(solution)/shard_map/gather | solution.py:96
  55.0 3.9 %copy.36 = bf16[2048,512]{0,1:T(8,128)(2,1)} copy(bf16[2048,512]{1,0:T(8,128)(2,1)} %param.33) | data formatting | bytes 4194304 | tf_op args[16]
  59.1 9.2 %gather_fusion.5 = bf16[2048,512]{1,0:T(8,128)(2,1)} fusion(bf16[640,512]{1,0:T(8,128)(2,1)S(1)} %constant_dynamic-update-slice_fusion, s32[2048]{0:T(1024)S(1)} %fusion.62), kind=kCustom, calls=%fused_computation.5 | custom fusion | bytes 4202496 | tf_op jit(solution)/shard_map/gather | solution.py:95
  68.4 3.3 %constant_dynamic-update-slice_fusion.7 = bf16[2048,1536]{1,0:T(8,128)(2,1)} fusion(bf16[2048,1536]{1,0:T(8,128)(2,1)} %constant_dynamic-update-slice_fusion.8, bf16[2048,512]{1,0:T(8,128)(2,1)} %gather_fusion.5), kind=kLoop, calls=%fused_computation.115 | loop fusion | bytes 4194304
  71.7 1.5 constant_dynamic-update-slice_fusion.6
  73.2 5.5 %fusion.83 = f32[2048,512]{1,0:T(8,128)S(1)} fusion(bf16[2048,1536]{1,0:T(8,128)(2,1)} %constant_dynamic-update-slice_fusion.6, bf16[1536,512]{1,0:T(8,128)(2,1)S(1)} %copy-done), kind=kOutput, calls=%fused_computation.157 | convolution fusion | flops 3221225472 | bytes 12058624 | tf_op jit(solution)/shard_map/jvp()/dot_general | solution.py:34
  78.8 1.6 fusion.79
  81.3 2.6 copy-done.7
  83.9 3.9 %add_convert_fusion = (bf16[2048,512]{0,1:T(8,128)(2,1)}, f32[2048,512]{0,1:T(8,128)}) fusion(bf16[2048,512]{0,1:T(8,128)(2,1)S(1)} %copy-done.7, f32[2048]{0:T(1024)S(1)} %fusion.64, f32[512]{0:T(512)S(1)} %copy-done.16, f32[2048]{0:T(1024)S(1)} %fusion.65, f32[2048,512]{0,1:T(8,128)S(1)} %get-tuple-element.66, f32[2048]{0:T(1024)S(1)} %broadcast_multiply_fusion), kind=kLoop, calls=%fused_computation.30 | loop fusion | flops 7340032 | bytes 12609536 | tf_op jit(solution)/shard_map/jvp()/convert_element_type | solution.py:38
  87.8 5.4 %copy.34 = f32[2048,512]{1,0:T(8,128)} copy(f32[2048,512]{0,1:T(8,128)} %get-tuple-element.53) | data formatting | bytes 8388608 | tf_op jit(solution)/shard_map/jvp()/mul | solution.py:37
  93.3 15.2 %scatter_custom_fusion = f32[256,512]{1,0:T(8,128)S(1)} fusion(s32[2048]{0:T(1024)S(1)} %copy-done.18, f32[2048,512]{1,0:T(8,128)} %copy.34, f32[]{:T(128)} %constant.10.clone.1), kind=kCustom, calls=%fused_computation.80 | custom fusion | flops 1048576 | bytes 524800 | tf_op jit(solution)/shard_map/scatter-add | solution.py:106
  108.5 1.7 convolution_add_fusion
  112.6 1.4 fusion.25
  114.5 1.8 fusion.18
  116.3 9.1 %gather_fusion.7 = f32[2048,512]{1,0:T(8,128)} fusion(f32[256,512]{1,0:T(8,128)S(1)} %slice_convert_fusion, s32[2048]{0:T(1024)S(1)} %fusion.63), kind=kCustom, calls=%fused_computation.7 | custom fusion | bytes 8396800 | tf_op jit(solution)/shard_map/gather | solution.py:112
  125.4 5.4 %copy.37 = f32[2048,512]{0,1:T(8,128)} copy(f32[2048,512]{1,0:T(8,128)} %gather_fusion.7) | data formatting | bytes 8388608 | tf_op jit(solution)/shard_map/gather | solution.py:112
  130.9 5.8 %multiply_reduce_fusion = (f32[512]{0:T(512)S(1)}, f32[2048]{0:T(1024)S(1)}) fusion(f32[2048,512]{0,1:T(8,128)} %copy-done.2, f32[2048]{0:T(1024)S(1)} %fusion.65, f32[2048]{0:T(1024)S(1)} %broadcast_multiply_fusion, f32[2048]{0:T(1024)S(1)} %fusion.64, f32[2048,512]{0,1:T(8,128)} %copy.37, bf16[2048,512]{0,1:T(8,128)(2,1)} %copy.36, f32[512]{0:T(512)S(1)} %copy-done.16), kind=kLoop, calls=%fused_computation.23 | loop fusion | flops 10483200 | bytes 10522624 | tf_op jit(solution)/shard_map/transpose(jvp())/reduce_sum | solution.py:28
  138.0 1.7 fusion.75
  140.4 2.7 fusion.81
  143.1 2.3 fusion.22
  145.6 5.1 %fusion.13 = f32[1536,512]{1,0:T(8,128)} fusion(bf16[2048,1536]{1,0:T(8,128)(2,1)S(1)} %bitcast.34, bf16[2048,512]{1,0:T(8,128)(2,1)S(1)} %get-tuple-element.70), kind=kOutput, calls=%fused_computation.41 | convolution fusion | flops 3222011904 | bytes 11534336 | tf_op jit(solution)/shard_map/transpose(jvp())/dot_general | solution.py:34
  150.8 7.0 %fusion.84 = bf16[2048,1536]{1,0:T(8,128)(2,1)} fusion(bf16[2048,512]{1,0:T(8,128)(2,1)} %copy-done.28, bf16[1536,512]{1,0:T(8,128)(2,1)S(1)} %copy-done), kind=kOutput, calls=%fused_computation.158 | convolution fusion | flops 3221225472 | bytes 9961472 | tf_op jit(solution)/shard_map/transpose(jvp())/dot_general | solution.py:34
  157.8 13.9 %scatter_custom_fusion.1 = f32[640,512]{1,0:T(8,128)S(1)} fusion(s32[2048]{0:T(1024)S(1)} %copy-done.17, bf16[2048,1536]{1,0:T(8,128)(2,1)} %fusion.84, f32[]{:T(128)} %constant.10.clone.1), kind=kCustom, calls=%fused_computation.26 | custom fusion | flops 2097152 | bytes 3408384 | tf_op jit(solution)/shard_map/scatter-add | solution.py:117
  173.5 9.5 %all-to-all-start.1 = ((bf16[128,2,512]{2,1,0:T(2,128)(2,1)}), bf16[128,2,512]{2,1,0:T(2,128)(2,1)S(1)}, u32[]{:S(2)}, u32[]{:S(2)}) async-start(bf16[128,2,512]{2,1,0:T(2,128)(2,1)} %convert_element_type.128), calls=%async_computation.1 | async-start | bytes 524288 | tf_op jit(solution)/shard_map/all_to_all | solution.py:140
  183.0 1.2 slice_add_fusion.1
  184.3 3.8 %slice_add_fusion = bf16[2048,512]{1,0:T(8,128)(2,1)} fusion(bf16[2048,512]{1,0:T(8,128)(2,1)} %param.33, bf16[2048,1536]{1,0:T(8,128)(2,1)} %fusion.84), kind=kLoop, calls=%fused_computation.42 | loop fusion | flops 1048576 | bytes 6291456 | tf_op jit(solution)/shard_map/transpose(jvp())/add_any | solution.py:33
  188.9 3.6 %collective-permute-start.4 = (bf16[32,512]{1,0:T(8,128)(2,1)S(1)}, bf16[32,512]{1,0:T(8,128)(2,1)S(1)}, u32[]{:S(2)}, u32[]{:S(2)}) collective-permute-start(bf16[32,512]{1,0:T(8,128)(2,1)S(1)} %get-tuple-element.57), channel_id=1, source_target_pairs={{0,16},{16,32},{32,48},{48,64},{64,80},{80,96},{96,112},{1,17},{17... | collective-permute-start | bytes 98312 | tf_op jit(solution)/shard_map/ppermute | solution.py:18
  192.5 1.9 collective-permute-start.5
  195.6 4.2 %collective-permute-start.7 = (bf16[32,512]{1,0:T(8,128)(2,1)S(1)}, bf16[32,512]{1,0:T(8,128)(2,1)S(1)}, u32[]{:S(2)}, u32[]{:S(2)}) collective-permute-start(bf16[32,512]{1,0:T(8,128)(2,1)S(1)} %get-tuple-element.55), channel_id=1, source_target_pairs={{1,0},{2,1},{3,2},{4,3},{5,4},{6,5},{7,6},{8,7},{9,8},{10,9},{11,1... | collective-permute-start | bytes 98312 | tf_op jit(solution)/shard_map/ppermute | solution.py:19
  200.8 15.4 %scatter_custom_fusion.2 = f32[256,512]{1,0:T(8,128)S(1)} fusion(f32[256,512]{1,0:T(8,128)S(1)} %slice_add_fusion.1, s32[2048]{0:T(1024)S(1)} %copy-done.18, bf16[2048,1536]{1,0:T(8,128)(2,1)} %fusion.84), kind=kCustom, calls=%fused_computation.24 | custom fusion | flops 2097152 | bytes 2621440 | tf_op jit(solution)/shard_map/scatter-add | solution.py:114
  216.1 3.9 %copy.38 = bf16[2048,512]{1,0:T(8,128)(2,1)} copy(bf16[2048,512]{0,1:T(8,128)(2,1)} %get-tuple-element.52) | data formatting | bytes 4194304
  220.1 62.9 %all-reduce = (f32[512]{0:T(512)}, f32[512]{0:T(512)}, f32[512]{0:T(512)}, f32[512]{0:T(512)}) all-reduce(f32[512]{0:T(512)S(1)} %get-tuple-element.69, f32[512]{0:T(512)S(1)} %get-tuple-element.36, f32[512]{0:T(512)S(1)} %get-tuple-element.71, f32[512]{0:T(512)S(1)} %get-tuple-element.38), channel_id=1, replica_groups=mesh['lat'=8,'lon'=16] {'lat','lon'}, use_global_device_ids=true, to_apply=%region_18.19 | all-reduce | flops 2048 | bytes 16384 | tf_op jit(solution)/shard_map/psum | solution.py:146
  287.2 2.3 scatter_fusion
  290.2 24.6 %all-reduce.4.cloned.1.call-done = (f32[1536,512]{1,0:T(8,128)}, f32[512,512]{1,0:T(8,128)}, f32[1024,512]{1,0:T(8,128)}, f32[512,512]{1,0:T(8,128)}) async-done(((f32[1536,512]{1,0:T(8,128)}, f32[512,512]{1,0:T(8,128)}, f32[1024,512]{1,0:T(8,128)}, f32[512,512]{1,0:T(8,128)}), (f32[1536,512]{1,0:T(8,128)}, f32[512,512]{1,0:T(8,128)}, f32[1024,512]{1,0:T(8,128)}, ...) | async-done | bytes 7340048 | tf_op jit(solution)/shard_map/psum | solution.py:146
  314.9 4.0 %copy.57 = f32[1536,512]{1,0:T(8,128)} copy(f32[1536,512]{1,0:T(8,128)} %get-tuple-element.81) | data formatting | bytes 6291456
  319.9 1.3 copy.59
  (125 shorter events, 20.6 us)
Async XLA Ops:
  7.2 66.0 %copy-start = (bf16[1536,512]{1,0:T(8,128)(2,1)S(1)}, bf16[1536,512]{1,0:T(8,128)(2,1)}, u32[]{:S(2)}) copy-start(bf16[1536,512]{1,0:T(8,128)(2,1)} %param.24) | copy-start | bytes 4718596
  7.2 30.8 %copy-start.1 = (bf16[256,512]{1,0:T(8,128)(2,1)S(1)}, bf16[256,512]{1,0:T(8,128)(2,1)}, u32[]{:S(2)}) copy-start(bf16[256,512]{1,0:T(8,128)(2,1)} %param.17) | copy-start | bytes 786436
  7.2 30.9 %copy-start.17 = (s32[2048]{0:T(1024)S(1)}, s32[2048]{0:T(1024)}, u32[]{:S(2)}) copy-start(s32[2048]{0:T(1024)} %param.21) | copy-start | bytes 24580
  9.7 49.2 %collective-permute-start = (bf16[32,512]{1,0:T(8,128)(2,1)S(1)}, bf16[32,512]{1,0:T(8,128)(2,1)S(1)}, u32[]{:S(2)}, u32[]{:S(2)}) collective-permute-start(bf16[32,512]{1,0:T(8,128)(2,1)S(1)} %gather_fusion), channel_id=1, source_target_pairs={{0,16},{16,32},{32,48},{48,64},{64,80},{80,96},{96,112},{1,17},{17... | collective-permute-start | bytes 98312 | tf_op jit(solution)/shard_map/ppermute | solution.py:18
  15.9 43.1 %collective-permute-start.1 = (bf16[32,512]{1,0:T(8,128)(2,1)S(1)}, bf16[32,512]{1,0:T(8,128)(2,1)S(1)}, u32[]{:S(2)}, u32[]{:S(2)}) collective-permute-start(bf16[32,512]{1,0:T(8,128)(2,1)S(1)} %gather_fusion.1), channel_id=1, source_target_pairs={{16,0},{32,16},{48,32},{64,48},{80,64},{96,80},{112,96},{17,1},{33... | collective-permute-start | bytes 98312 | tf_op jit(solution)/shard_map/ppermute | solution.py:19
  19.4 39.5 %collective-permute-start.2 = (bf16[32,512]{1,0:T(8,128)(2,1)S(1)}, bf16[32,512]{1,0:T(8,128)(2,1)S(1)}, u32[]{:S(2)}, u32[]{:S(2)}) collective-permute-start(bf16[32,512]{1,0:T(8,128)(2,1)S(1)} %gather_fusion.2), channel_id=1, source_target_pairs={{0,1},{1,2},{2,3},{3,4},{4,5},{5,6},{6,7},{7,8},{8,9},{9,10},{10,1... | collective-permute-start | bytes 98312 | tf_op jit(solution)/shard_map/ppermute | solution.py:18
  22.4 18.8 %copy-start.18 = (s32[2048]{0:T(1024)S(1)}, s32[2048]{0:T(1024)}, u32[]{:S(2)}) copy-start(s32[2048]{0:T(1024)} %param.20) | copy-start | bytes 24580
  22.4 36.6 %collective-permute-start.3 = (bf16[32,512]{1,0:T(8,128)(2,1)S(1)}, bf16[32,512]{1,0:T(8,128)(2,1)S(1)}, u32[]{:S(2)}, u32[]{:S(2)}) collective-permute-start(bf16[32,512]{1,0:T(8,128)(2,1)S(1)} %gather_fusion.3), channel_id=1, source_target_pairs={{1,0},{2,1},{3,2},{4,3},{5,4},{6,5},{7,6},{8,7},{9,8},{10,9},{11,1... | collective-permute-start | bytes 98312 | tf_op jit(solution)/shard_map/ppermute | solution.py:19
  31.4 27.6 %all-to-all-start = ((bf16[128,2,512]{2,1,0:T(2,128)(2,1)}), bf16[128,2,512]{2,1,0:T(2,128)(2,1)S(1)}, u32[]{:S(2)}, u32[]{:S(2)}) async-start(bf16[128,2,512]{2,1,0:T(2,128)(2,1)} %reshape.255), calls=%async_computation | async-start | bytes 524288 | tf_op jit(solution)/shard_map/all_to_all | solution.py:82
  37.8 277.0 %all-reduce.4.cloned.1.call-start = ((), (), s32[]{:S(2)}) async-start(), calls=%async_computation.2 | async-start | bytes 14680064 | tf_op jit(solution)/shard_map/psum | solution.py:146
  68.4 3.3 %copy-start.6 = (bf16[2048,512]{1,0:T(8,128)(2,1)S(1)}, bf16[2048,512]{1,0:T(8,128)(2,1)}, u32[]{:S(2)}) copy-start(bf16[2048,512]{1,0:T(8,128)(2,1)} %gather_fusion.6) | copy-start | bytes 6291460
  73.2 5.5 %copy-start.21 = (bf16[512,512]{1,0:T(8,128)(2,1)S(1)}, bf16[512,512]{1,0:T(8,128)(2,1)}, u32[]{:S(2)}) copy-start(bf16[512,512]{1,0:T(8,128)(2,1)} %param.26) | copy-start | bytes 1572868
  73.2 5.6 %copy-start.24 = (f32[512]{0:T(512)S(1)}, f32[512]{0:T(512)}, u32[]{:S(2)}) copy-start(f32[512]{0:T(512)} %param.25) | copy-start | bytes 6148
  78.7 2.0 copy-start.25
  80.8 7.0 %copy-start.2 = (f32[2048,512]{0,1:T(8,128)}, f32[2048,512]{0,1:T(8,128)S(1)}, u32[]{:S(2)}) copy-start(f32[2048,512]{0,1:T(8,128)S(1)} %get-tuple-element.66) | copy-start | bytes 12582916
  80.8 3.1 copy-start.7
  80.8 3.1 copy-start.16
  87.8 20.7 %copy-start.23 = (f32[512]{0:T(512)S(1)}, f32[512]{0:T(512)}, u32[]{:S(2)}) copy-start(f32[512]{0:T(512)} %param.29) | copy-start | bytes 6148
  87.8 22.4 %copy-start.20 = (bf16[512,512]{1,0:T(8,128)(2,1)S(1)}, bf16[512,512]{1,0:T(8,128)(2,1)}, u32[]{:S(2)}) copy-start(bf16[512,512]{1,0:T(8,128)(2,1)} %param.30) | copy-start | bytes 1572868
  93.3 17.6 %copy-start.9 = (bf16[256,512]{1,0:T(8,128)(2,1)S(1)}, bf16[256,512]{1,0:T(8,128)(2,1)}, u32[]{:S(2)}) copy-start(bf16[256,512]{1,0:T(8,128)(2,1)} %param.32) | copy-start | bytes 786436
  93.3 17.6 %copy-start.19 = (f32[512]{0:T(512)S(1)}, f32[512]{0:T(512)}, u32[]{:S(2)}) copy-start(f32[512]{0:T(512)} %param.31) | copy-start | bytes 6148
  111.2 2.8 copy-start.13
  114.5 11.0 %copy-start.11 = (bf16[256,1024]{1,0:T(8,128)(2,1)}, bf16[256,1024]{1,0:T(8,128)(2,1)S(1)}, u32[]{:S(2)}) copy-start(bf16[256,1024]{1,0:T(8,128)(2,1)S(1)} %fusion.85) | copy-start | bytes 1572868
  130.9 5.8 %copy-start.3 = (f32[2048,512]{0,1:T(8,128)S(1)}, f32[2048,512]{0,1:T(8,128)}, u32[]{:S(2)}) copy-start(f32[2048,512]{0,1:T(8,128)} %copy-done.2) | copy-start | bytes 12582916
  130.9 6.5 %copy-start.4 = (f32[2048,512]{0,1:T(8,128)S(1)}, f32[2048,512]{0,1:T(8,128)}, u32[]{:S(2)}) copy-start(f32[2048,512]{0,1:T(8,128)} %copy.37) | copy-start | bytes 12582916
  130.9 7.1 %copy-start.5 = (bf16[2048,512]{0,1:T(8,128)(2,1)S(1)}, bf16[2048,512]{0,1:T(8,128)(2,1)}, u32[]{:S(2)}) copy-start(bf16[2048,512]{0,1:T(8,128)(2,1)} %copy.36) | copy-start | bytes 6291460
  138.0 1.7 copy-start.22
  138.0 2.4 copy-start.26
  140.3 2.7 copy-start.27
  140.3 5.1 %slice-start = ((s8[6291456]{0:T(1024)(128)(4,1)}), s8[4194304]{0:T(1024)(128)(4,1)S(1)}, s32[]{:S(2)}) async-start(s8[6291456]{0:T(1024)(128)(4,1)} %bitcast.33), calls=%async_computation.3 | async-start | bytes 8388608
  143.1 2.4 copy-start.28
  143.1 2.5 slice-start.1
  171.7 1.9 copy-start.8
  171.8 0.9 copy-start.10
  173.5 113.6 %all-to-all-start.1 = ((bf16[128,2,512]{2,1,0:T(2,128)(2,1)}), bf16[128,2,512]{2,1,0:T(2,128)(2,1)S(1)}, u32[]{:S(2)}, u32[]{:S(2)}) async-start(bf16[128,2,512]{2,1,0:T(2,128)(2,1)} %convert_element_type.128), calls=%async_computation.1 | async-start | bytes 524288 | tf_op jit(solution)/shard_map/all_to_all | solution.py:140
  188.9 94.1 %collective-permute-start.4 = (bf16[32,512]{1,0:T(8,128)(2,1)S(1)}, bf16[32,512]{1,0:T(8,128)(2,1)S(1)}, u32[]{:S(2)}, u32[]{:S(2)}) collective-permute-start(bf16[32,512]{1,0:T(8,128)(2,1)S(1)} %get-tuple-element.57), channel_id=1, source_target_pairs={{0,16},{16,32},{32,48},{48,64},{64,80},{80,96},{96,112},{1,17},{17... | collective-permute-start | bytes 98312 | tf_op jit(solution)/shard_map/ppermute | solution.py:18
  192.5 90.5 %collective-permute-start.5 = (bf16[32,512]{1,0:T(8,128)(2,1)S(1)}, bf16[32,512]{1,0:T(8,128)(2,1)S(1)}, u32[]{:S(2)}, u32[]{:S(2)}) collective-permute-start(bf16[32,512]{1,0:T(8,128)(2,1)S(1)} %get-tuple-element.56), channel_id=1, source_target_pairs={{16,0},{32,16},{48,32},{64,48},{80,64},{96,80},{112,96},{17,1},{33... | collective-permute-start | bytes 98312 | tf_op jit(solution)/shard_map/ppermute | solution.py:19
  194.5 90.6 %collective-permute-start.6 = (bf16[32,512]{1,0:T(8,128)(2,1)S(1)}, bf16[32,512]{1,0:T(8,128)(2,1)S(1)}, u32[]{:S(2)}, u32[]{:S(2)}) collective-permute-start(bf16[32,512]{1,0:T(8,128)(2,1)S(1)} %get-tuple-element.54), channel_id=1, source_target_pairs={{0,1},{1,2},{2,3},{3,4},{4,5},{5,6},{6,7},{7,8},{8,9},{9,10},{10,1... | collective-permute-start | bytes 98312 | tf_op jit(solution)/shard_map/ppermute | solution.py:18
  195.6 89.4 %collective-permute-start.7 = (bf16[32,512]{1,0:T(8,128)(2,1)S(1)}, bf16[32,512]{1,0:T(8,128)(2,1)S(1)}, u32[]{:S(2)}, u32[]{:S(2)}) collective-permute-start(bf16[32,512]{1,0:T(8,128)(2,1)S(1)} %get-tuple-element.55), channel_id=1, source_target_pairs={{1,0},{2,1},{3,2},{4,3},{5,4},{6,5},{7,6},{8,7},{9,8},{10,9},{11,1... | collective-permute-start | bytes 98312 | tf_op jit(solution)/shard_map/ppermute | solution.py:19
  314.9 4.0 %copy-start.15 = (f32[512,512]{1,0:T(8,128)S(1)}, f32[512,512]{1,0:T(8,128)}, u32[]{:S(2)}) copy-start(f32[512,512]{1,0:T(8,128)} %get-tuple-element.83) | copy-start | bytes 3145732
  314.9 5.0 %copy-start.12 = (f32[1024,512]{1,0:T(8,128)S(1)}, f32[1024,512]{1,0:T(8,128)}, u32[]{:S(2)}) copy-start(f32[1024,512]{1,0:T(8,128)} %get-tuple-element.85) | copy-start | bytes 6291460
  318.9 2.3 copy-start.14
Sparse Core Ops, SparseCore 0:
  150.9 163.9 all-reduce.3
where the time goes:
time: 334 us; the launch traced here: 329 us
  local copies, waits for them, and re-layouts  84.6 us (25%)
  other arithmetic  71.2 us (21%)
  blocking collectives  62.9 us (19%)
  starting transfers between devices  39.9 us (12%)
  matrix products  30.4 us (9%)
  waiting for transfers between devices  24.7 us (7%)
  between operations  15.8 us (5%)
    psum x1, blocking collectives, shards(): summed = lax.psum(every_grad, ('lat', 'lon'))  62.9 us
    unnamed x77, local copies, waits for them, and re-layouts  32.4 us
    psum x1, waiting for transfers between devices, shards(): summed = lax.psum(every_grad, ('lat', 'lon'))  24.6 us
    dot_general x3, matrix products, edge_update(): jnp.dot(joined, weight_in, preferred_element_type=jnp.float32) + bias_in  17.7 us
    scatter-add x1, other arithmetic, shards(): jax.ops.segment_sum(from_receive.astype(jnp.float32), receiver, node_rows...  15.4 us
    scatter-add x1, other arithmetic, shards(): jax.ops.segment_sum(message, receiver, node_rows, indices_are_sorted=True)  15.2 us
    gather x2, local copies, waits for them, and re-layouts, shards(): from_gathered.astype(jnp.float32)[receiver]  14.6 us
    scatter-add x1, other arithmetic, shards(): jax.ops.segment_sum(from_send.astype(jnp.float32), sender, node_rows + 4...  13.9 us
  transfers between devices with their start and end apart: 11, of which 1 were waited for; matrix products, arithmetic and copies ran while one was open for 26% of the time, Pallas kernels for 0%

commit v1 on v0

v1 whole, which is shorter than its diff:
```python
import functools

import jax
import jax.numpy as jnp
from jax import lax
from jax.experimental import pallas as pl
from jax.experimental.pallas import tpu as pltpu
from jax.sharding import PartitionSpec as P

EPS = 1e-05
F32 = jnp.float32
BF16 = jnp.bfloat16
MESH = pl.DeviceIdType.MESH
D = 512
N = 256
EDGES = 2048
HALO = 128
FAR = 256
TABLE = HALO + FAR
SLOTS = N + TABLE
CHUNK = 512
CHUNKS = EDGES // CHUNK
GROWS = 3584
FLAT = 4 * GROWS
HALF = FLAT // 2
SECTIONS = (48, 32, 32)
OFFSETS = (0, 64 * 48, 64 * 80)
VMEM_LIMIT = 60 * 1024 * 1024


def nn(a, b):
    return jnp.dot(a, b, preferred_element_type=F32)


def nt(a, b):
    return lax.dot_general(a, b, (((1,), (1,)), ((), ())), preferred_element_type=F32)


def tn(a, b):
    return lax.dot_general(a, b, (((0,), (0,)), ((), ())), preferred_element_type=F32)


def iota(shape, dim):
    return lax.broadcasted_iota(jnp.int32, shape, dim)


def one_hot(mask):
    return jnp.where(mask, 1.0, 0.0).astype(BF16)


def index_columns(row):
    count = row.shape[1] // 128
    parts = [jnp.broadcast_to(row[:, q * 128 : (q + 1) * 128], (128, 128)).T for q in range(count)]
    return parts[0] if count == 1 else jnp.concatenate(parts, axis=0)


def one_hot_rows(columns, first, blocks):
    lane = iota(columns.shape, 1)
    parts = [one_hot(columns == lane + (first + 128 * k)) for k in range(blocks)]
    return jnp.concatenate(parts, axis=1)


def position():
    return lax.axis_index("lat"), lax.axis_index("lon")


def entry_barrier(b, t):
    barrier = pltpu.get_barrier_semaphore()
    for step in range(1, 8):
        pl.semaphore_signal(barrier, inc=1, device_id=(lax.rem(b + step, 8), t), device_id_type=MESH)
    for step in range(1, 16):
        pl.semaphore_signal(barrier, inc=1, device_id=(b, lax.rem(t + step, 16)), device_id_type=MESH)
    pl.semaphore_wait(barrier, 22)


def send(src, dst, send_sem, recv_sem, device):
    pltpu.make_async_remote_copy(
        src_ref=src, dst_ref=dst, send_sem=send_sem, recv_sem=recv_sem, device_id=device, device_id_type=MESH
    ).start()


def wait_bytes(ref, sem):
    pltpu.make_async_copy(ref, ref, sem).wait()


def halo_swap(src, land, b, t, send_sem, recv_sem):
    down, up = (lax.rem(b + 7, 8), t), (lax.rem(b + 1, 8), t)
    left, right = (b, lax.rem(t + 15, 16)), (b, lax.rem(t + 1, 16))

    def part(ref, k):
        return ref.at[pl.ds(32 * k, 32)]

    @pl.when(b > 0)
    def _():
        send(part(src, 0), part(land, 1), send_sem.at[0], recv_sem.at[1], down)

    @pl.when(b < 7)
    def _():
        send(part(src, 1), part(land, 0), send_sem.at[1], recv_sem.at[0], up)

    send(part(src, 2), part(land, 3), send_sem.at[2], recv_sem.at[3], left)
    send(part(src, 3), part(land, 2), send_sem.at[3], recv_sem.at[2], right)


def halo_wait(src, land, b, send_sem, recv_sem):
    def part(ref, k):
        return ref.at[pl.ds(32 * k, 32)]

    @pl.when(b > 0)
    def _():
        wait_bytes(part(src, 0), send_sem.at[0])
        wait_bytes(part(land, 0), recv_sem.at[0])

    @pl.when(b < 7)
    def _():
        wait_bytes(part(src, 1), send_sem.at[1])
        wait_bytes(part(land, 1), recv_sem.at[1])

    for k in (2, 3):
        wait_bytes(part(src, k), send_sem.at[k])
        wait_bytes(part(land, k), recv_sem.at[k])


def swap_order(rows_major, cols_major):
    count = rows_major * cols_major * 2
    row, col = iota((count, count), 0), iota((count, count), 1)
    p, q, c = row // (2 * cols_major), lax.rem(row // 2, cols_major), lax.rem(row, 2)
    return one_hot(col == q * (2 * rows_major) + p * 2 + c)


def fetch_kernel(nodes, index, table, out_s, land_h, land_1, far_2, land_2, hs, hr, s1, r1, s2, r2):
    b, t = position()
    columns = index_columns(index[...])
    rows = nn(one_hot_rows(columns, 0, 2), nodes[...])
    out_s[...] = rows.astype(BF16)

    @pl.when(b == 0)
    def _():
        land_h[0:32, :] = jnp.zeros((32, D), BF16)

    @pl.when(b == 7)
    def _():
        land_h[32:64, :] = jnp.zeros((32, D), BF16)

    entry_barrier(b, t)
    for step in range(1, 16):
        peer = lax.rem(t + step, 16)
        send(
            out_s.at[pl.ds(pl.multiple_of(HALO + peer * 16, 16), 16)],
            land_1.at[pl.ds(pl.multiple_of(t * 16, 16), 16)],
            s1,
            r1,
            (b, peer),
        )
    halo_swap(out_s, land_h, b, t, hs, hr)
    land_1[pl.ds(pl.multiple_of(t * 16, 16), 16), :] = out_s[
        pl.ds(pl.multiple_of(HALO + t * 16, 16), 16), :
    ]
    wait_bytes(land_1.at[pl.ds(0, 240)], r1)
    far_2[...] = nn(swap_order(8, 16), land_1[...]).astype(BF16)
    for step in range(1, 8):
        peer = lax.rem(b + step, 8)
        send(
            far_2.at[pl.ds(pl.multiple_of(peer * 32, 16), 32)],
            land_2.at[pl.ds(pl.multiple_of(b * 32, 16), 32)],
            s2,
            r2,
            (peer, t),
        )
    land_2[pl.ds(pl.multiple_of(b * 32, 16), 32), :] = far_2[pl.ds(pl.multiple_of(b * 32, 16), 32), :]
    halo_wait(out_s, land_h, b, hs, hr)
    wait_bytes(out_s.at[pl.ds(0, 240)], s1)
    wait_bytes(land_2.at[pl.ds(0, 224)], r2)
    wait_bytes(far_2.at[pl.ds(0, 224)], s2)
    table[0:HALO, :] = land_h[...]
    table[HALO:TABLE, :] = land_2[...]


def norm_parts(values):
    mean = jnp.mean(values, axis=-1, keepdims=True)
    centered = values - mean
    variance = jnp.mean(centered * centered, axis=-1, keepdims=True)
    scale = lax.rsqrt(variance + EPS)
    return centered * scale, scale


def norm_back(grad, hat, scale):
    first = jnp.mean(grad, axis=-1, keepdims=True)
    second = jnp.mean(grad * hat, axis=-1, keepdims=True)
    return scale * (grad - first - hat * second)


def silu_parts(values):
    gate = 0.5 * jnp.tanh(0.5 * values) + 0.5
    active = values * gate
    return active, gate + active * (1.0 - gate)


def put_flat(ref, first, values):
    rows = values.shape[0]
    for k in range(4):
        ref[k * GROWS + first : k * GROWS + first + rows, :] = values[:, 128 * k : 128 * (k + 1)]


def put_small(ref, first, values):
    for k in range(4):
        ref[first + k : first + k + 1, :] = values[:, 128 * k : 128 * (k + 1)]


def step_kernel(
    count, sidx, ridx, nodes, table, cot_nodes, eb, eg, nb, ng,
    edges_h, cot_edges_h, ewi_h, ewo_h, nwi_h, nwo_h,
    node_out, totals, slots, flat, small, edge_out_h, grad_edges_h,
    edges, cots, ewi, ewo, nwi, nwo, rhs, ewoT, ewiT, active_s, slope_s, hat_s, scale_s, ohr_s,
    gathered, g_in, g_out, g_slots, g_bias, g_gain, eout, gout,
    in_sems, cot_sems, w_sems, out_sems,
):
    def block(ref, i):
        return ref.at[pl.ds(pl.multiple_of(i * CHUNK, CHUNK), CHUNK)]

    weights = [(ewi_h, ewi), (ewo_h, ewo), (nwi_h, nwi), (nwo_h, nwo)]

    def weight_copy(k):
        return pltpu.make_async_copy(weights[k][0], weights[k][1], w_sems.at[k])

    weight_copy(0).start()
    weight_copy(1).start()
    for i in range(CHUNKS):
        pltpu.make_async_copy(block(edges_h, i), block(edges, i), in_sems.at[i]).start()
    weight_copy(2).start()
    weight_copy(3).start()
    for i in range(CHUNKS):
        pltpu.make_async_copy(block(cot_edges_h, i), block(cots, i), cot_sems.at[i]).start()

    gathered[...] = jnp.zeros_like(gathered)
    g_in[...] = jnp.zeros_like(g_in)
    g_out[...] = jnp.zeros_like(g_out)
    g_slots[...] = jnp.zeros_like(g_slots)
    g_bias[...] = jnp.zeros_like(g_bias)
    g_gain[...] = jnp.zeros_like(g_gain)

    weight_copy(0).wait()
    rhs[0:D, :] = ewi[0:D, :]
    rhs[D : D + N, :] = nn(nodes[...], ewi[D : 2 * D, :]).astype(BF16)
    rhs[D + N : D + SLOTS, :] = nn(table[...], ewi[D : 2 * D, :]).astype(BF16)
    rhs[D + SLOTS :, :] = nn(nodes[...], ewi[2 * D :, :]).astype(BF16)
    ewiT[...] = ewi[0:D, :].T
    weight_copy(1).wait()
    ewoT[...] = ewo[...].T
    live = count[0]

    def rows_of(i):
        return pl.ds(pl.multiple_of(i * CHUNK, CHUNK), CHUNK)

    def live_mask(i):
        return jnp.where(iota((CHUNK, 1), 0) + i * CHUNK < live, 1.0, 0.0)

    def forward(i, carry):
        rows = rows_of(i)
        pltpu.make_async_copy(block(edges_h, i), block(edges, i), in_sems.at[i]).wait()
        r_row = ridx[:, rows]
        ohs = one_hot_rows(index_columns(sidx[:, rows]), 0, 5)
        ohr = one_hot_rows(index_columns(r_row), 0, 2)
        ohr_s[rows, :] = ohr
        e = edges[rows, :]
        first = nn(jnp.concatenate([e, ohs, ohr], axis=1), rhs[...]) + eb[...]
        active, slope = silu_parts(first)
        active = active.astype(BF16)
        active_s[rows, :] = active
        slope_s[rows, :] = slope.astype(BF16)
        hat, scale = norm_parts(nn(active, ewo[...]))
        hat_s[rows, :] = hat.astype(BF16)
        scale_s[rows, :] = scale
        message = hat * eg[...] * live_mask(i)
        eout[rows, :] = (e.astype(F32) + message).astype(BF16)
        pltpu.make_async_copy(block(eout, i), block(edge_out_h, i), out_sems.at[0, i]).start()
        ohr_t = one_hot(iota((N, CHUNK), 0) == r_row)
        gathered[...] += nn(ohr_t, message.astype(BF16))
        return carry

    lax.fori_loop(0, CHUNKS, forward, 0)

    weight_copy(2).wait()
    weight_copy(3).wait()
    x = nodes[...]
    got = gathered[...].astype(BF16)
    first = nn(x, nwi[0:D, :]) + nn(got, nwi[D:, :]) + nb[...]
    active, slope = silu_parts(first)
    active = active.astype(BF16)
    hat, scale = norm_parts(nn(active, nwo[...]))
    node_out[...] = (x.astype(F32) + hat * ng[...]).astype(BF16)
    cot = cot_nodes[...].astype(F32)
    put_small(small, 12, jnp.sum(cot * hat, axis=0, keepdims=True))
    d_second = norm_back(cot * ng[...], hat, scale).astype(BF16)
    put_flat(flat, 3072, tn(active, d_second).astype(BF16))
    d_first = nt(d_second, nwo[...]) * slope
    put_small(small, 8, jnp.sum(d_first, axis=0, keepdims=True))
    d_first = d_first.astype(BF16)
    put_flat(flat, 2048, tn(x, d_first).astype(BF16))
    put_flat(flat, 2560, tn(got, d_first).astype(BF16))
    totals[...] = nt(d_first, nwi[0:D, :]) + cot
    from_gathered = nt(d_first, nwi[D:, :]).astype(BF16)

    def backward(i, carry):
        rows = rows_of(i)
        pltpu.make_async_copy(block(cot_edges_h, i), block(cots, i), cot_sems.at[i]).wait()
        ce = cots[rows, :].astype(F32)
        hat = hat_s[rows, :].astype(F32)
        d_message = (ce + nn(ohr_s[rows, :], from_gathered)) * live_mask(i)
        g_gain[...] += jnp.sum(d_message * hat, axis=0, keepdims=True)
        d_second = norm_back(d_message * eg[...], hat, scale_s[rows, :]).astype(BF16)
        g_out[...] += tn(active_s[rows, :], d_second)
        d_first = nn(d_second, ewoT[...]) * slope_s[rows, :].astype(F32)
        g_bias[...] += jnp.sum(d_first, axis=0, keepdims=True)
        d_first = d_first.astype(BF16)
        gout[rows, :] = (nn(d_first, ewiT[...]) + ce).astype(BF16)
        pltpu.make_async_copy(block(gout, i), block(grad_edges_h, i), out_sems.at[1, i]).start()
        g_in[...] += tn(edges[rows, :], d_first)
        oh_t = jnp.concatenate(
            [one_hot(iota((SLOTS, CHUNK), 0) == sidx[:, rows]), one_hot(iota((N, CHUNK), 0) == ridx[:, rows])],
            axis=0,
        )
        g_slots[...] += nn(oh_t, d_first)
        return carry

    lax.fori_loop(0, CHUNKS, backward, 0)

    put_small(small, 0, g_bias[...])
    put_small(small, 4, g_gain[...])
    put_flat(flat, 0, g_in[...].astype(BF16))
    put_flat(flat, 1536, g_out[...].astype(BF16))
    gs = g_slots[...].astype(BF16)
    put_flat(
        flat,
        512,
        (tn(nodes[...], gs[0:N, :]) + tn(table[...], gs[N:SLOTS, :])).astype(BF16),
    )
    put_flat(flat, 1024, tn(nodes[...], gs[SLOTS:, :]).astype(BF16))
    totals[...] += nt(gs[0:N, :], ewi[D : 2 * D, :]) + nt(gs[SLOTS:, :], ewi[2 * D :, :])
    slots[...] = nt(gs[N:SLOTS, :], ewi[D : 2 * D, :]).astype(BF16)
    for i in range(CHUNKS):
        pltpu.make_async_copy(block(eout, i), block(edge_out_h, i), out_sems.at[0, i]).wait()
        pltpu.make_async_copy(block(gout, i), block(grad_edges_h, i), out_sems.at[1, i]).wait()


def reduce_kernel(
    flat, small, slots, index, totals, grad_nodes, result, small_out,
    half, land_c, land_x, land_y, land_z, mid_x, mid_y, sm, sm_land,
    land_h, land_1, far_2, land_2,
    hs, hr, s1, r1, s2, r2, ss, sr, gs, gr,
):
    b, t = position()
    core, x = lax.rem(b, 2), b // 2
    y, z = lax.rem(t, 4), t // 4
    entry_barrier(b, t)

    for step in range(1, 8):
        peer = lax.rem(b + step, 8)
        send(
            slots.at[pl.ds(pl.multiple_of(HALO + peer * 32, 16), 32)],
            land_1.at[pl.ds(pl.multiple_of(b * 32, 16), 32)],
            s1,
            r1,
            (peer, t),
        )
    halo_swap(slots, land_h, b, t, hs, hr)
    land_1[pl.ds(pl.multiple_of(b * 32, 16), 32), :] = slots[
        pl.ds(pl.multiple_of(HALO + b * 32, 16), 32), :
    ]

    @pl.when(b == 0)
    def _():
        land_h[0:32, :] = jnp.zeros((32, D), BF16)

    @pl.when(b == 7)
    def _():
        land_h[32:64, :] = jnp.zeros((32, D), BF16)

    def pick(axis, values):
        return jnp.where(axis == 0, values[0], jnp.where(axis == 1, values[1], values[2]))

    def axis_of(k, stage):
        return lax.rem(core + (k + stage), 3)

    def place(k, stage):
        return pick(axis_of(k, stage), (x, y, z))

    def mate(k, stage, step):
        axis = axis_of(k, stage)
        other = lax.rem(pick(axis, (x, y, z)) + step, 4)
        ox, oy, oz = (jnp.where(axis == a, other, v) for a, v in enumerate((x, y, z)))
        return other, (ox * 2 + core, oz * 4 + oy)

    core_mate = (x * 2 + (1 - core), t)

    def rows(start, size):
        return pl.ds(pl.multiple_of(start, 16), size)

    lands = (land_x, land_y, land_z)
    for k, s in enumerate(SECTIONS):
        send(
            flat.at[rows((1 - core) * HALF + OFFSETS[k], 64 * s)],
            land_c.at[rows(OFFSETS[k], 64 * s)],
            gs.at[0, k],
            gr.at[0, k],
            core_mate,
        )
    send(small, sm_land.at[0], ss.at[0], sr.at[0], core_mate)
    for k, s in enumerate(SECTIONS):
        mine = rows(OFFSETS[k], 64 * s)
        wait_bytes(land_c.at[mine], gr.at[0, k])
        total = flat[rows(core * HALF + OFFSETS[k], 64 * s), :].astype(F32) + land_c[mine, :].astype(F32)
        half[mine, :] = total.astype(BF16)
        for step in range(1, 4):
            other, device = mate(k, 0, step)
            send(
                half.at[rows(OFFSETS[k] + other * (16 * s), 16 * s)],
                land_x.at[rows((OFFSETS[k] // 64 * 16) * 3 + (step - 1) * 16 * s, 16 * s)],
                gs.at[1, k],
                gr.at[1, k],
                device,
            )
    wait_bytes(small, ss.at[0])
    wait_bytes(sm_land.at[0], sr.at[0])
    sm[0] = small[...] + sm_land[0]

    def small_stage(stage):
        own = (x, y, z)[stage]
        for step in range(1, 4):
            other = lax.rem(own + step, 4)
            ox, oy, oz = (other if a == stage else v for a, v in enumerate((x, y, z)))
            send(
                sm.at[stage],
                sm_land.at[1 + 4 * stage + own],
                ss.at[1 + stage],
                sr.at[1 + stage],
                (ox * 2 + core, oz * 4 + oy),
            )

    def small_finish(stage):
        own = (x, y, z)[stage]
        sm_land[1 + 4 * stage + own] = sm[stage]
        wait_bytes(sm_land.at[pl.ds(0, 3)], sr.at[1 + stage])
        wait_bytes(sm_land.at[pl.ds(0, 3)], ss.at[1 + stage])
        first = 1 + 4 * stage
        total = sm_land[first] + sm_land[first + 1] + sm_land[first + 2] + sm_land[first + 3]
        if stage < 2:
            sm[stage + 1] = total
        else:
            small_out[...] = total

    small_stage(0)
    wait_bytes(land_1.at[pl.ds(0, 224)], r1)
    far_2[...] = nn(swap_order(16, 8), land_1[...]).astype(BF16)
    for step in range(1, 16):
        peer = lax.rem(t + step, 16)
        send(
            far_2.at[rows(peer * 16, 16)],
            land_2.at[rows(t * 16, 16)],
            s2,
            r2,
            (b, peer),
        )
    land_2[rows(t * 16, 16), :] = far_2[rows(t * 16, 16), :]

    sources = (half, mid_x, mid_y)
    starts = (OFFSETS, tuple(o // 4 for o in OFFSETS), tuple(o // 16 for o in OFFSETS))
    for stage in range(3):
        part = (16, 4, 1)[stage]
        source, land = sources[stage], lands[stage]
        for k, s in enumerate(SECTIONS):
            size = part * s
            first = (OFFSETS[k] // 64 * part) * 3
            wait_bytes(land.at[rows(first, 3 * size)], gr.at[1 + stage, k])
            own = place(k, stage)
            total = source[rows(starts[stage][k] + own * size, size), :].astype(F32)
            for j in range(3):
                total = total + land[rows(first + j * size, size), :].astype(F32)
            total = total.astype(BF16)
            if stage < 2:
                target = sources[stage + 1]
                begin = starts[stage + 1][k]
                target[rows(begin, size), :] = total
                for step in range(1, 4):
                    other, device = mate(k, stage + 1, step)
                    piece = size // 4
                    next_first = (OFFSETS[k] // 64 * (part // 4)) * 3
                    send(
                        target.at[rows(begin + other * piece, piece)],
                        lands[stage + 1].at[rows(next_first + (step - 1) * piece, piece)],
                        gs.at[2 + stage, k],
                        gr.at[2 + stage, k],
                        device,
                    )
            else:
                result[final_rows(core, k, s, place, rows, 3), :] = total
                spread(result, core, k, s, place, mate, rows, 2, gs, gr)
        small_finish(stage)
        if stage < 2:
            small_stage(stage + 1)

    for stage in (2, 1, 0):
        for k, s in enumerate(SECTIONS):
            size = (16, 4, 1)[stage] * s
            wait_bytes(result.at[pl.ds(0, 3 * size)], gr.at[4 + stage, k])
            if stage > 0:
                spread(result, core, k, s, place, mate, rows, stage - 1, gs, gr)
            else:
                whole = result.at[rows(core * HALF + OFFSETS[k], 64 * s)]
                send(whole, whole, gs.at[7, k], gr.at[7, k], core_mate)

    halo_wait(slots, land_h, b, hs, hr)
    wait_bytes(slots.at[pl.ds(0, 224)], s1)
    wait_bytes(land_2.at[pl.ds(0, 240)], r2)
    wait_bytes(far_2.at[pl.ds(0, 240)], s2)
    back = jnp.concatenate([land_h[...], land_2[...]], axis=0)
    spread_rows = one_hot(iota((N, TABLE), 0) == index[...])
    grad_nodes[...] = (totals[...] + nn(spread_rows, back)).astype(BF16)

    for k, s in enumerate(SECTIONS):
        wait_bytes(result.at[pl.ds(0, 64 * s)], gr.at[7, k])
        wait_bytes(result.at[pl.ds(0, 64 * s)], gs.at[7, k])
        wait_bytes(flat.at[pl.ds(0, 64 * s)], gs.at[0, k])
        for stage in range(3):
            size = (16, 4, 1)[stage] * s
            wait_bytes(result.at[pl.ds(0, 3 * size)], gs.at[1 + stage, k])
            wait_bytes(result.at[pl.ds(0, 3 * size)], gs.at[4 + stage, k])


def final_rows(core, k, s, place, rows, depth):
    start = core * HALF + OFFSETS[k]
    size = 64 * s
    for stage in range(depth):
        size //= 4
        start = start + place(k, stage) * size
    return rows(start, size)


def spread(result, core, k, s, place, mate, rows, stage, gs, gr):
    block = result.at[final_rows(core, k, s, place, rows, stage + 1)]
    for step in range(1, 4):
        _, device = mate(k, stage, step)
        send(block, block, gs.at[4 + stage, k], gr.at[4 + stage, k], device)


def widen_kernel(flat, ewi, ewo, nwi, nwo):
    i = pl.program_id(0)

    def write(ref):
        for k in range(4):
            ref[:, 128 * k : 128 * (k + 1)] = flat[k].astype(F32)

    pl.when(i < 3)(lambda: write(ewi))
    pl.when(i == 3)(lambda: write(ewo))
    pl.when((i == 4) | (i == 5))(lambda: write(nwi))
    pl.when(i == 6)(lambda: write(nwo))


def vmem(count):
    return [pl.BlockSpec(memory_space=pltpu.VMEM)] * count


def shape(rows, dtype=BF16, width=D):
    return jax.ShapeDtypeStruct((rows, width), dtype)


def fetch(nodes, index):
    dma = pltpu.SemaphoreType.DMA
    return pl.pallas_call(
        fetch_kernel,
        out_shape=shape(TABLE),
        in_specs=vmem(2),
        out_specs=vmem(1)[0],
        scratch_shapes=[
            pltpu.VMEM((TABLE, D), BF16),
            pltpu.VMEM((HALO, D), BF16),
            pltpu.VMEM((FAR, D), BF16),
            pltpu.VMEM((FAR, D), BF16),
            pltpu.VMEM((FAR, D), BF16),
            dma((4,)),
            dma((4,)),
            dma(()),
            dma(()),
            dma(()),
            dma(()),
        ],
        compiler_params=pltpu.CompilerParams(
            collective_id=0, has_side_effects=True, vmem_limit_bytes=16 * 1024 * 1024
        ),
    )(nodes, index)


def compute(count, sidx, ridx, nodes, table, cot_nodes, eb, eg, nb, ng, edges, cots, ewi, ewo, nwi, nwo):
    dma = pltpu.SemaphoreType.DMA
    hbm = pl.BlockSpec(memory_space=pl.ANY)
    v = pltpu.VMEM
    return pl.pallas_call(
        step_kernel,
        out_shape=(
            shape(N),
            shape(N, F32),
            shape(TABLE),
            shape(FLAT, BF16, 128),
            shape(16, F32, 128),
            shape(EDGES),
            shape(EDGES),
        ),
        in_specs=[pl.BlockSpec(memory_space=pltpu.SMEM)] + vmem(9) + [hbm] * 6,
        out_specs=tuple(vmem(5) + [hbm] * 2),
        scratch_shapes=[
            v((EDGES, D), BF16),
            v((EDGES, D), BF16),
            v((3 * D, D), BF16),
            v((D, D), BF16),
            v((2 * D, D), BF16),
            v((D, D), BF16),
            v((D + SLOTS + N, D), BF16),
            v((D, D), BF16),
            v((D, D), BF16),
            v((EDGES, D), BF16),
            v((EDGES, D), BF16),
            v((EDGES, D), BF16),
            v((EDGES, 1), F32),
            v((EDGES, N), BF16),
            v((N, D), F32),
            v((D, D), F32),
            v((D, D), F32),
            v((SLOTS + N, D), F32),
            v((1, D), F32),
            v((1, D), F32),
            v((EDGES, D), BF16),
            v((EDGES, D), BF16),
            dma((CHUNKS,)),
            dma((CHUNKS,)),
            dma((4,)),
            dma((2, CHUNKS)),
        ],
        compiler_params=pltpu.CompilerParams(vmem_limit_bytes=VMEM_LIMIT),
    )(count, sidx, ridx, nodes, table, cot_nodes, eb, eg, nb, ng, edges, cots, ewi, ewo, nwi, nwo)


def reduce(flat, small, slots, index, totals):
    dma = pltpu.SemaphoreType.DMA
    v = pltpu.VMEM
    return pl.pallas_call(
        reduce_kernel,
        out_shape=(shape(N), shape(FLAT, BF16, 128), shape(16, F32, 128)),
        in_specs=vmem(5),
        out_specs=tuple(vmem(3)),
        scratch_shapes=[
            v((HALF, 128), BF16),
            v((HALF, 128), BF16),
            v((HALF // 4 * 3, 128), BF16),
            v((HALF // 16 * 3, 128), BF16),
            v((HALF // 64 * 3, 128), BF16),
            v((HALF // 4, 128), BF16),
            v((HALF // 16, 128), BF16),
            v((3, 16, 128), F32),
            v((13, 16, 128), F32),
            v((HALO, D), BF16),
            v((FAR, D), BF16),
            v((FAR, D), BF16),
            v((FAR, D), BF16),
            dma((4,)),
            dma((4,)),
            dma(()),
            dma(()),
            dma(()),
            dma(()),
            dma((4,)),
            dma((4,)),
            dma((8, 3)),
            dma((8, 3)),
        ],
        compiler_params=pltpu.CompilerParams(
            collective_id=1, has_side_effects=True, vmem_limit_bytes=48 * 1024 * 1024
        ),
    )(flat, small, slots, index, totals)


def widen(flat):
    def spec(least, most):
        return pl.BlockSpec((512, 512), lambda i: (jnp.clip(i - least, 0, most), 0))

    return pl.pallas_call(
        widen_kernel,
        grid=(7,),
        out_shape=(shape(1536, F32), shape(512, F32), shape(1024, F32), shape(512, F32)),
        in_specs=[pl.BlockSpec((4, 512, 128), lambda i: (0, i, 0))],
        out_specs=(spec(0, 2), spec(3, 0), spec(4, 1), spec(6, 0)),
    )(flat.reshape(4, GROWS, 128))


def shards(
    node_latents, edge_latents, edge_count, receiver, sender, halo_send, far_send,
    edge_weight_in, edge_bias, edge_weight_out, edge_gain,
    node_weight_in, node_bias, node_weight_out, node_gain, cot_nodes, cot_edges,
):
    halo = halo_send[0]
    far = far_send[0].reshape(8, 16, 2).transpose(1, 0, 2).reshape(1, FAR)
    index = jnp.concatenate([halo.reshape(1, HALO), far], axis=1)
    table = fetch(node_latents, index)
    node_out, totals, slots, flat, small, edge_out, grad_edges = compute(
        edge_count, sender.reshape(1, EDGES), receiver.reshape(1, EDGES),
        node_latents, table, cot_nodes,
        edge_bias.reshape(1, D), edge_gain.reshape(1, D), node_bias.reshape(1, D), node_gain.reshape(1, D),
        edge_latents, cot_edges, edge_weight_in, edge_weight_out, node_weight_in, node_weight_out,
    )
    grad_nodes, flat, small = reduce(flat, small, slots, index, totals)
    g_ewi, g_ewo, g_nwi, g_nwo = widen(flat)
    small = small.reshape(4, D)
    return (
        node_out, edge_out, grad_nodes, grad_edges,
        g_ewi, small[0], g_ewo, small[1], g_nwi, small[2], g_nwo, small[3],
    )


def solution(mesh):
    split = ("lat", "lon")
    rows, flat = P(split, None), P(split)
    cube, whole = P(split, None, None), P()
    return jax.shard_map(
        shards,
        mesh=mesh,
        in_specs=(rows, rows, flat, flat, flat, cube, cube) + (whole,) * 8 + (rows, rows),
        out_specs=(rows, rows, rows, rows) + (whole,) * 8,
        check_vma=False,
    )
```

time: 334 us -> 113 us (0.34); the launches traced: 329 us -> 112 us
  Pallas kernels: 0 us -> 102 us
  local copies, waits for them, and re-layouts: 84.6 us -> 9.3 us
  other arithmetic: 71.2 us -> 0 us
  blocking collectives: 62.9 us -> 0 us
  starting transfers between devices: 39.9 us -> 0 us
  matrix products: 30.4 us -> 0 us
  waiting for transfers between devices: 24.7 us -> 0 us
  between operations: 15.8 us -> 1.36 us
    pallas_call x0 -> x4, Pallas kernels: none -> 102 us  [the longest x1 47 us: reduce(): pl.pallas_call(reduce_kernel, out_shape=(shape(N), shape(FLAT, BF16, 128)...]
    psum x1 -> x0, blocking collectives: 62.9 us -> none  [shards(): summed = lax.psum(every_grad, ('lat', 'lon'))]
    scatter-add x8 -> x0, other arithmetic: 50.8 us -> none  [the longest x1 15.4 us: shards(): jax.ops.segment_sum(from_receive.astype(jnp.float32), receiver, node_rows...]
    gather x9 -> x0, local copies, waits for them, and re-layouts: 41.6 us -> none  [the longest x2 14.6 us: shards(): from_gathered.astype(jnp.float32)[receiver]]
    dot_general x12 -> x0, matrix products: 30.4 us -> none  [the longest x3 17.7 us: edge_update(): jnp.dot(joined, weight_in, preferred_element_type=jnp.float32) + bias_in]
    unnamed x77 -> x14, local copies, waits for them, and re-layouts: 32.4 us -> 6.91 us
    psum x1 -> x0, waiting for transfers between devices: 24.6 us -> none  [shards(): summed = lax.psum(every_grad, ('lat', 'lon'))]
    ppermute x8 -> x0, starting transfers between devices: 23.7 us -> none  [the longest x4 13.1 us: padded(): after = lax.ppermute(first, axis, down)]
  transfers between devices with their start and end apart: 11 -> 0, of which waited for: 1 -> 0; matrix products, arithmetic and copies ran while one was open for 26% -> 0% of each run, Pallas kernels for 0% -> 0%
where the time goes in v1:
time: 113 us; the launch traced here: 112 us
  Pallas kernels  102 us (90%)
  local copies, waits for them, and re-layouts  9.3 us (8%)
  between operations  1.36 us (1%)
    pallas_call x1, Pallas kernels, reduce(): pl.pallas_call(reduce_kernel, out_shape=(shape(N), shape(FLAT, BF16, 128)...  47 us
    pallas_call x1, Pallas kernels, compute(): pl.pallas_call(step_kernel, out_shape=(shape(N), shape(N, F32), shape(TAB...  27.5 us
    pallas_call x1, Pallas kernels, fetch(): pl.pallas_call(fetch_kernel, out_shape=shape(TABLE), in_specs=vmem(2), ou...  19.5 us
    pallas_call x1, Pallas kernels, widen(): pl.pallas_call(widen_kernel, grid=(7,), out_shape=(shape(1536, F32), shap...  7.67 us
    unnamed x14, local copies, waits for them, and re-layouts  6.91 us

profile of v1, /device:TPU:1, one launch (start us, length us, event | category | flops | bytes accessed | tf_op | source)
XLA Modules:
  0.0 112.3 jit_solution(3669356334735184959)
XLA Ops:
  1.3 0.8 reshape_squeeze.6
  2.1 0.8 reshape_squeeze.7
  2.8 0.1 copy.30
  2.9 0.1 reshape.59
  3.1 0.0 copy-start.2
  3.1 0.9 copy-done.2
  4.1 19.5 %shard_map.256.table = bf16[384,512]{1,0:T(8,128)(2,1)S(1)} custom-call(bf16[256,512]{1,0:T(8,128)(2,1)S(1)} %copy-done.2, s32[1,384]{1,0:T(1,128)S(1)} %constant_dynamic-update-slice_fusion.index), custom_call_target="tpu_custom_call" | custom-call | tf_op jit(solution)/shard_map/pallas_call | solution.py:569
  23.6 0.0 copy-start.1
  23.6 0.7 copy-done.1
  24.3 27.5 %shard_map.257 = (bf16[256,512]{1,0:T(8,128)(2,1)}, f32[256,512]{1,0:T(8,128)}, bf16[384,512]{1,0:T(8,128)(2,1)}, bf16[14336,128]{1,0:T(8,128)(2,1)}, f32[16,128...) custom-call(s32[1]{0:T(128)S(6)} %copy.33.count, s32[1,2048]{1,0:T(1,128)} %bitcast.20, ...), custom_call_target="tpu_custom_call" | custom-call | tf_op jit(solution)/shard_map/pallas_call | solution.py:597
  51.8 0.0 copy-start.3
  51.8 1.0 copy-done.3
  52.8 0.0 copy-start.4
  52.8 1.0 copy-done.4
  53.8 0.0 copy-start.5
  53.8 0.7 copy-done.5
  54.5 47.0 %shard_map.258 = (bf16[256,512]{1,0:T(8,128)(2,1)S(1)}, bf16[14336,128]{1,0:T(8,128)(2,1)S(1)}, f32[16,128]{1,0:T(8,128)S(1)}) custom-call(bf16[14336,128]{1,0:T(8,128)(2,1)} %get-tuple-element.28.flat, f32[16,128]{1,0:T(8,128)S(1)} %copy-done.5, bf16[384,512]{1,0:T(8,128)(2,1)S(1)} %copy-done.4, s32[1,384]{1,0:T(1,128)S(1)} %constant_dynamic-update-slice_fusion.index, ...), custom_call_target="tpu_custom_call" | custom-call | tf_op jit(solution)/shard_map/pallas_call | solution.py:645
  101.6 0.0 copy-start
  101.6 1.8 %copy-done = bf16[14336,128]{1,0:T(8,128)(2,1)} copy-done((bf16[14336,128]{1,0:T(8,128)(2,1)}, bf16[14336,128]{1,0:T(8,128)(2,1)S(1)}, u32[]{:S(2)}) %copy-start) | copy-done | bytes 3670040
  103.3 0.6 slice_bitcast_fusion
  103.9 7.7 %shard_map.259 = (f32[1536,512]{1,0:T(8,128)}, f32[512,512]{1,0:T(8,128)}, f32[1024,512]{1,0:T(8,128)}, f32[512,512]{1,0:T(8,128)}) custom-call(bf16[4,3584,128]{2,1,0:T(8,128)(2,1)} %bitcast.18), custom_call_target="tpu_custom_call" | custom-call | tf_op jit(solution)/shard_map/pallas_call | solution.py:685
  111.6 0.7 copy.34
  (2 shorter events, 0.0 us)
Async XLA Ops:
  3.1 1.0 copy-start.2
  23.6 0.7 copy-start.1
  51.8 1.0 copy-start.3
  52.8 1.0 copy-start.4
  53.8 0.7 copy-start.5
  101.6 1.8 %copy-start = (bf16[14336,128]{1,0:T(8,128)(2,1)}, bf16[14336,128]{1,0:T(8,128)(2,1)S(1)}, u32[]{:S(2)}) copy-start(bf16[14336,128]{1,0:T(8,128)(2,1)S(1)} %get-tuple-element.34) | copy-start | bytes 11010052

commit v2 on v1

v2 whole, which is shorter than its diff:
```python
import functools

import jax
import jax.numpy as jnp
from jax import lax
from jax.experimental import pallas as pl
from jax.experimental.pallas import tpu as pltpu
from jax.sharding import PartitionSpec as P

EPS = 1e-05
F32 = jnp.float32
BF16 = jnp.bfloat16
MESH = pl.DeviceIdType.MESH
D = 512
N = 256
EDGES = 2048
HALO = 128
FAR = 256
TABLE = HALO + FAR
SLOTS = N + TABLE
CHUNK = 512
CHUNKS = EDGES // CHUNK
EDGE_ROWS = 2048
NODE_ROWS = 1536
EDGE_PARTS = (32, 16, 16)
NODE_PARTS = (16, 16, 16)
VMEM_LIMIT = 63 * 1024 * 1024


def nn(a, b):
    return jnp.dot(a, b, preferred_element_type=F32)


def nt(a, b):
    return lax.dot_general(a, b, (((1,), (1,)), ((), ())), preferred_element_type=F32)


def tn(a, b):
    return lax.dot_general(a, b, (((0,), (0,)), ((), ())), preferred_element_type=F32)


def iota(shape, dim):
    return lax.broadcasted_iota(jnp.int32, shape, dim)


def one_hot(mask):
    return jnp.where(mask, 1.0, 0.0).astype(BF16)


def index_columns(row):
    count = row.shape[1] // 128
    parts = [jnp.broadcast_to(row[:, q * 128 : (q + 1) * 128], (128, 128)).T for q in range(count)]
    return parts[0] if count == 1 else jnp.concatenate(parts, axis=0)


def one_hot_rows(columns, first, blocks):
    lane = iota(columns.shape, 1)
    parts = [one_hot(columns == lane + (first + 128 * k)) for k in range(blocks)]
    return jnp.concatenate(parts, axis=1)


def position():
    return lax.axis_index("lat"), lax.axis_index("lon")


def greet(b, t):
    barrier = pltpu.get_barrier_semaphore()
    for step in range(1, 8):
        pl.semaphore_signal(barrier, inc=1, device_id=(lax.rem(b + step, 8), t), device_id_type=MESH)
    for step in range(1, 16):
        pl.semaphore_signal(barrier, inc=1, device_id=(b, lax.rem(t + step, 16)), device_id_type=MESH)


def send(src, dst, send_sem, recv_sem, device):
    pltpu.make_async_remote_copy(
        src_ref=src, dst_ref=dst, send_sem=send_sem, recv_sem=recv_sem, device_id=device, device_id_type=MESH
    ).start()


def wait_bytes(ref, sem):
    pltpu.make_async_copy(ref, ref, sem).wait()


def halo_swap(src, land, b, t, send_sem, recv_sem):
    down, up = (lax.rem(b + 7, 8), t), (lax.rem(b + 1, 8), t)
    left, right = (b, lax.rem(t + 15, 16)), (b, lax.rem(t + 1, 16))

    def part(ref, k):
        return ref.at[pl.ds(32 * k, 32)]

    @pl.when(b > 0)
    def _():
        send(part(src, 0), part(land, 1), send_sem.at[0], recv_sem.at[1], down)

    @pl.when(b < 7)
    def _():
        send(part(src, 1), part(land, 0), send_sem.at[1], recv_sem.at[0], up)

    send(part(src, 2), part(land, 3), send_sem.at[2], recv_sem.at[3], left)
    send(part(src, 3), part(land, 2), send_sem.at[3], recv_sem.at[2], right)


def halo_wait(src, land, b, send_sem, recv_sem):
    def part(ref, k):
        return ref.at[pl.ds(32 * k, 32)]

    @pl.when(b > 0)
    def _():
        wait_bytes(part(src, 0), send_sem.at[0])
        wait_bytes(part(land, 0), recv_sem.at[0])

    @pl.when(b < 7)
    def _():
        wait_bytes(part(src, 1), send_sem.at[1])
        wait_bytes(part(land, 1), recv_sem.at[1])

    for k in (2, 3):
        wait_bytes(part(src, k), send_sem.at[k])
        wait_bytes(part(land, k), recv_sem.at[k])


def swap_order(rows_major, cols_major):
    count = rows_major * cols_major * 2
    row, col = iota((count, count), 0), iota((count, count), 1)
    p, q, c = row // (2 * cols_major), lax.rem(row // 2, cols_major), lax.rem(row, 2)
    return one_hot(col == q * (2 * rows_major) + p * 2 + c)


def norm_parts(values):
    mean = jnp.mean(values, axis=-1, keepdims=True)
    centered = values - mean
    variance = jnp.mean(centered * centered, axis=-1, keepdims=True)
    scale = lax.rsqrt(variance + EPS)
    return centered * scale, scale


def norm_back(grad, hat, scale):
    first = jnp.mean(grad, axis=-1, keepdims=True)
    second = jnp.mean(grad * hat, axis=-1, keepdims=True)
    return scale * (grad - first - hat * second)


def silu_parts(values):
    gate = 0.5 * jnp.tanh(0.5 * values) + 0.5
    active = values * gate
    return active, gate + active * (1.0 - gate)


def put_flat(ref, first, values):
    rows, total = values.shape[0], ref.shape[0] // 4
    for k in range(4):
        ref[k * total + first : k * total + first + rows, :] = values[:, 128 * k : 128 * (k + 1)]


def put_small(ref, first, values):
    for k in range(4):
        ref[first + k : first + k + 1, :] = values[:, 128 * k : 128 * (k + 1)]


def rows16(start, size):
    return pl.ds(pl.multiple_of(start, 16), size)


def pick(axis, values):
    return jnp.where(axis == 0, values[0], jnp.where(axis == 1, values[1], values[2]))


class Place:
    def __init__(self):
        self.b, self.t = position()
        self.core = lax.rem(self.b, 2)
        self.xyz = (self.b // 2, lax.rem(self.t, 4), self.t // 4)
        self.core_mate = (self.xyz[0] * 2 + (1 - self.core), self.t)

    def axis(self, k, stage):
        return lax.rem(self.core + (k + stage), 3)

    def own(self, k, stage):
        return pick(self.axis(k, stage), self.xyz)

    def mate(self, k, stage, step):
        axis = self.axis(k, stage)
        other = lax.rem(pick(axis, self.xyz) + step, 4)
        ox, oy, oz = (jnp.where(axis == a, other, v) for a, v in enumerate(self.xyz))
        return other, (ox * 2 + self.core, oz * 4 + oy)


class AllReduce:
    def __init__(self, place, parts, flat, result, half, land_c, lands, mids, gs, gr):
        self.at, self.parts, self.flat, self.result = place, parts, flat, result
        self.half, self.land_c, self.lands = half, land_c, lands
        self.sources = (half,) + mids
        self.gs, self.gr = gs, gr
        self.units = [sum(parts[:k]) for k in range(len(parts))]
        self.base = place.core * (flat.shape[0] // 2)
        self.other_base = (1 - place.core) * (flat.shape[0] // 2)

    def core_send(self):
        for k, s in enumerate(self.parts):
            first = 64 * self.units[k]
            send(
                self.flat.at[rows16(self.other_base + first, 64 * s)],
                self.land_c.at[rows16(first, 64 * s)],
                self.gs.at[0, k],
                self.gr.at[0, k],
                self.at.core_mate,
            )

    def send_parts(self, k, stage):
        size = (16, 4, 1)[stage] * self.parts[k]
        first = (64, 16, 4)[stage] * self.units[k]
        land_first = (16, 4, 1)[stage] * self.units[k] * 3
        for step in range(1, 4):
            other, device = self.at.mate(k, stage, step)
            send(
                self.sources[stage].at[rows16(first + other * size, size)],
                self.lands[stage].at[rows16(land_first + (step - 1) * size, size)],
                self.gs.at[1 + stage, k],
                self.gr.at[1 + stage, k],
                device,
            )

    def core_sum(self):
        for k, s in enumerate(self.parts):
            mine = rows16(64 * self.units[k], 64 * s)
            wait_bytes(self.land_c.at[mine], self.gr.at[0, k])
            own = self.flat[rows16(self.base + 64 * self.units[k], 64 * s), :]
            self.half[mine, :] = (own.astype(F32) + self.land_c[mine, :].astype(F32)).astype(BF16)
            self.send_parts(k, 0)

    def axis_sum(self, stage):
        for k, s in enumerate(self.parts):
            size = (16, 4, 1)[stage] * s
            first = (64, 16, 4)[stage] * self.units[k]
            land_first = (16, 4, 1)[stage] * self.units[k] * 3
            land = self.lands[stage]
            wait_bytes(land.at[rows16(land_first, 3 * size)], self.gr.at[1 + stage, k])
            total = self.sources[stage][rows16(first + self.at.own(k, stage) * size, size), :].astype(F32)
            for j in range(3):
                total = total + land[rows16(land_first + j * size, size), :].astype(F32)
            total = total.astype(BF16)
            if stage < 2:
                self.sources[stage + 1][rows16((16, 4)[stage] * self.units[k], size), :] = total
                self.send_parts(k, stage + 1)
            else:
                self.result[self.final(k, 3), :] = total
                self.spread(k, 2)

    def final(self, k, depth):
        start, size = self.base + 64 * self.units[k], 64 * self.parts[k]
        for stage in range(depth):
            size //= 4
            start = start + self.at.own(k, stage) * size
        return rows16(start, size)

    def spread(self, k, stage):
        block = self.result.at[self.final(k, stage + 1)]
        for step in range(1, 4):
            _, device = self.at.mate(k, stage, step)
            send(block, block, self.gs.at[4 + stage, k], self.gr.at[4 + stage, k], device)

    def back(self, stage):
        for k, s in enumerate(self.parts):
            size = (16, 4, 1)[stage] * s
            wait_bytes(self.result.at[pl.ds(0, 3 * size)], self.gr.at[4 + stage, k])
            if stage > 0:
                self.spread(k, stage - 1)
            else:
                whole = self.result.at[self.final(k, 0)]
                send(whole, whole, self.gs.at[7, k], self.gr.at[7, k], self.at.core_mate)

    def finish(self):
        for k, s in enumerate(self.parts):
            wait_bytes(self.result.at[pl.ds(0, 64 * s)], self.gr.at[7, k])
            wait_bytes(self.result.at[pl.ds(0, 64 * s)], self.gs.at[7, k])
            wait_bytes(self.flat.at[pl.ds(0, 64 * s)], self.gs.at[0, k])
            for stage in range(3):
                size = (16, 4, 1)[stage] * s
                wait_bytes(self.result.at[pl.ds(0, 3 * size)], self.gs.at[1 + stage, k])
                wait_bytes(self.result.at[pl.ds(0, 3 * size)], self.gs.at[4 + stage, k])


class SmallSum:
    def __init__(self, place, small, out, sums, land, ss, sr):
        self.at, self.small, self.out, self.sums, self.land = place, small, out, sums, land
        self.ss, self.sr = ss, sr

    def core_send(self):
        send(self.small, self.land.at[0], self.ss.at[0], self.sr.at[0], self.at.core_mate)

    def core_sum(self):
        wait_bytes(self.small, self.ss.at[0])
        wait_bytes(self.land.at[0], self.sr.at[0])
        self.sums[0] = self.small[...] + self.land[0]
        self.axis_send(0)

    def axis_send(self, stage):
        own = self.at.xyz[stage]
        for step in range(1, 4):
            other = lax.rem(own + step, 4)
            ox, oy, oz = (other if a == stage else v for a, v in enumerate(self.at.xyz))
            send(
                self.sums.at[stage],
                self.land.at[1 + 4 * stage + own],
                self.ss.at[1 + stage],
                self.sr.at[1 + stage],
                (ox * 2 + self.at.core, oz * 4 + oy),
            )

    def axis_sum(self, stage):
        first = 1 + 4 * stage
        self.land[first + self.at.xyz[stage]] = self.sums[stage]
        wait_bytes(self.land.at[pl.ds(0, 3)], self.sr.at[1 + stage])
        wait_bytes(self.land.at[pl.ds(0, 3)], self.ss.at[1 + stage])
        total = self.land[first] + self.land[first + 1] + self.land[first + 2] + self.land[first + 3]
        if stage < 2:
            self.sums[stage + 1] = total
            self.axis_send(stage + 1)
        else:
            self.out[...] = total


def step_kernel(
    count, halo_send_h, far_send_h, sidx_h, ridx_h, nodes_h, cot_nodes_h, eb_h, eg_h, nb_h, ng_h,
    edges_h, cot_edges_h, ewi_h, ewo_h, nwi_h, nwo_h,
    node_out, grad_nodes, edge_sum, node_sum, small_out, edge_out_h, grad_edges_h,
    halo_send, far_send, sidx, ridx, nodes, cot_nodes, eb, eg, nb, ng,
    edges, cots, ewi, ewo, nwi, nwo, rhs, rhs_far, ewoT, ewiT,
    first_s, active_s, slope_s, scale_s, ohr_s,
    picks, order, gathered, g_in, g_out, g_slots, g_bias, g_gain, totals, slots, small,
    out_s, table, land_1, far_2, edge_flat, node_flat,
    e_half, e_land_c, e_land_x, e_land_y, e_land_z, e_mid_x, e_mid_y,
    n_half, n_land_c, n_land_x, n_land_y, n_land_z, n_mid_x, n_mid_y,
    sm, sm_land, halo_back, land_1b, far_2b, land_2b,
    early_sems, in_sems, cot_sems, w_sems, out_sems,
    hs, hr, s1, r1, s2, r2, bhs, bhr, bs1, br1, bs2, br2, ss, sr, egs, egr, ngs, ngr,
):
    at = Place()
    b, t = at.b, at.t
    early = [
        pltpu.make_async_copy(source, target, early_sems.at[k])
        for k, (source, target) in enumerate(
            (
                (nodes_h, nodes), (halo_send_h, halo_send), (far_send_h, far_send), (sidx_h, sidx), (ridx_h, ridx),
                (eb_h, eb), (eg_h, eg), (nb_h, nb), (ng_h, ng), (cot_nodes_h, cot_nodes),
            )
        )
    ]
    for copy in early:
        copy.start()
    greet(b, t)

    def block(ref, i):
        return ref.at[pl.ds(pl.multiple_of(i * CHUNK, CHUNK), CHUNK)]

    weights = [(ewi_h, ewi), (ewo_h, ewo), (nwi_h, nwi), (nwo_h, nwo)]

    def weight_copy(k):
        return pltpu.make_async_copy(weights[k][0], weights[k][1], w_sems.at[k])

    weight_copy(0).start()
    for i in range(CHUNKS):
        pltpu.make_async_copy(block(edges_h, i), block(edges, i), in_sems.at[i]).start()
    for k in range(1, 4):
        weight_copy(k).start()
    for i in range(CHUNKS):
        pltpu.make_async_copy(block(cot_edges_h, i), block(cots, i), cot_sems.at[i]).start()

    for copy in early:
        copy.wait()
    x = nodes[...]
    halo_list = jnp.concatenate([halo_send[0, k : k + 1, :] for k in range(4)], axis=1)
    picks[0:HALO, :] = one_hot_rows(index_columns(halo_list), 0, 2)
    for c in range(2):
        wanted = index_columns(far_send[0, c : c + 1, :])
        picks[HALO + 128 * c : HALO + 128 * (c + 1), :] = one_hot_rows(wanted, 0, 2)
    out_s[0:HALO, :] = nn(picks[0:HALO, :], x).astype(BF16)
    far_rows = nn(picks[HALO:TABLE, :], x).astype(BF16)
    row, col = iota((FAR, FAR), 0), iota((FAR, FAR), 1)
    peer = lax.rem(col, 128)
    order[...] = one_hot(
        (lax.rem(row, 2) == col // 128) & (lax.rem(row // 2, 8) == peer // 16) & (row // 16 == lax.rem(peer, 16))
    )
    out_s[HALO:TABLE, :] = nn(order[...], far_rows).astype(BF16)

    @pl.when(b == 0)
    def _():
        table[0:32, :] = jnp.zeros((32, D), BF16)

    @pl.when(b == 7)
    def _():
        table[32:64, :] = jnp.zeros((32, D), BF16)

    pl.semaphore_wait(pltpu.get_barrier_semaphore(), 22)
    for step in range(1, 16):
        peer = lax.rem(t + step, 16)
        send(
            out_s.at[rows16(HALO + peer * 16, 16)], land_1.at[rows16(t * 16, 16)], s1, r1, (b, peer)
        )
    halo_swap(out_s, table, b, t, hs, hr)
    land_1[rows16(t * 16, 16), :] = out_s[rows16(HALO + t * 16, 16), :]

    gathered[...] = jnp.zeros_like(gathered)
    g_in[...] = jnp.zeros_like(g_in)
    g_out[...] = jnp.zeros_like(g_out)
    g_slots[...] = jnp.zeros_like(g_slots)
    g_bias[...] = jnp.zeros_like(g_bias)
    g_gain[...] = jnp.zeros_like(g_gain)

    weight_copy(0).wait()
    rhs[0:D, :] = ewi[0:D, :]
    rhs[D : D + N, :] = nn(x, ewi[D : 2 * D, :]).astype(BF16)
    rhs[D + N :, :] = nn(x, ewi[2 * D :, :]).astype(BF16)
    ewiT[...] = ewi[0:D, :].T
    live = count[0]

    def rows_of(i):
        return pl.ds(pl.multiple_of(i * CHUNK, CHUNK), CHUNK)

    def live_mask(i):
        return jnp.where(iota((CHUNK, 1), 0) + i * CHUNK < live, 1.0, 0.0)

    def local_part(i, carry):
        rows = rows_of(i)
        pltpu.make_async_copy(block(edges_h, i), block(edges, i), in_sems.at[i]).wait()
        own = one_hot_rows(index_columns(sidx[:, rows]), 0, 2)
        ohr = one_hot_rows(index_columns(ridx[:, rows]), 0, 2)
        ohr_s[rows, :] = ohr
        first_s[rows, :] = nn(jnp.concatenate([edges[rows, :], own, ohr], axis=1), rhs[...]) + eb[...]
        return carry

    lax.fori_loop(0, CHUNKS // 2, local_part, 0)
    wait_bytes(land_1.at[pl.ds(0, 240)], r1)
    far_2[...] = nn(swap_order(8, 16), land_1[...]).astype(BF16)
    for step in range(1, 8):
        peer = lax.rem(b + step, 8)
        send(
            far_2.at[rows16(peer * 32, 32)],
            table.at[rows16(HALO + b * 32, 32)],
            s2,
            r2,
            (peer, t),
        )
    table[rows16(HALO + b * 32, 32), :] = far_2[rows16(b * 32, 32), :]
    lax.fori_loop(CHUNKS // 2, CHUNKS, local_part, 0)
    weight_copy(1).wait()
    ewoT[...] = ewo[...].T
    halo_wait(out_s, table, b, hs, hr)
    wait_bytes(out_s.at[pl.ds(0, 240)], s1)
    wait_bytes(table.at[pl.ds(0, 224)], r2)
    wait_bytes(far_2.at[pl.ds(0, 224)], s2)
    rhs_far[...] = nn(table[...], ewi[D : 2 * D, :]).astype(BF16)

    def forward(i, carry):
        rows = rows_of(i)
        far = one_hot_rows(index_columns(sidx[:, rows]), N, 3)
        active, slope = silu_parts(first_s[rows, :] + nn(far, rhs_far[...]))
        active = active.astype(BF16)
        active_s[rows, :] = active
        slope_s[rows, :] = slope.astype(BF16)
        hat, scale = norm_parts(nn(active, ewo[...]))
        first_s[rows, :] = hat
        scale_s[rows, :] = scale
        message = hat * eg[...] * live_mask(i)
        ohr_t = one_hot(iota((N, CHUNK), 0) == ridx[:, rows])
        gathered[...] += nn(ohr_t, message.astype(BF16))
        return carry

    lax.fori_loop(0, CHUNKS, forward, 0)

    weight_copy(2).wait()
    weight_copy(3).wait()
    got = gathered[...].astype(BF16)
    first = nn(x, nwi[0:D, :]) + nn(got, nwi[D:, :]) + nb[...]
    active, slope = silu_parts(first)
    active = active.astype(BF16)
    hat, scale = norm_parts(nn(active, nwo[...]))
    node_out[...] = (x.astype(F32) + hat * ng[...]).astype(BF16)
    cot = cot_nodes[...].astype(F32)
    put_small(small, 12, jnp.sum(cot * hat, axis=0, keepdims=True))
    d_second = norm_back(cot * ng[...], hat, scale).astype(BF16)
    put_flat(node_flat, 1024, tn(active, d_second).astype(BF16))
    d_first = nt(d_second, nwo[...]) * slope
    put_small(small, 8, jnp.sum(d_first, axis=0, keepdims=True))
    d_first = d_first.astype(BF16)
    put_flat(node_flat, 0, tn(x, d_first).astype(BF16))
    put_flat(node_flat, 512, tn(got, d_first).astype(BF16))
    totals[...] = nt(d_first, nwi[0:D, :]) + cot
    from_gathered = nt(d_first, nwi[D:, :]).astype(BF16)

    node_ar = AllReduce(
        at, NODE_PARTS, node_flat, node_sum, n_half, n_land_c, (n_land_x, n_land_y, n_land_z),
        (n_mid_x, n_mid_y), ngs, ngr,
    )
    edge_ar = AllReduce(
        at, EDGE_PARTS, edge_flat, edge_sum, e_half, e_land_c, (e_land_x, e_land_y, e_land_z),
        (e_mid_x, e_mid_y), egs, egr,
    )
    small_ar = SmallSum(at, small, small_out, sm, sm_land, ss, sr)
    node_ar.core_send()

    def backward(i, carry):
        rows = rows_of(i)
        pltpu.make_async_copy(block(cot_edges_h, i), block(cots, i), cot_sems.at[i]).wait()
        ce = cots[rows, :].astype(F32)
        hat = first_s[rows, :]
        d_message = (ce + nn(ohr_s[rows, :], from_gathered)) * live_mask(i)
        g_gain[...] += jnp.sum(d_message * hat, axis=0, keepdims=True)
        d_second = norm_back(d_message * eg[...], hat, scale_s[rows, :]).astype(BF16)
        g_out[...] += tn(active_s[rows, :], d_second)
        d_first = nn(d_second, ewoT[...]) * slope_s[rows, :].astype(F32)
        g_bias[...] += jnp.sum(d_first, axis=0, keepdims=True)
        d_first = d_first.astype(BF16)
        slope_s[rows, :] = d_first
        g_in[...] += tn(edges[rows, :], d_first)
        oh_t = jnp.concatenate(
            [one_hot(iota((SLOTS, CHUNK), 0) == sidx[:, rows]), one_hot(iota((N, CHUNK), 0) == ridx[:, rows])],
            axis=0,
        )
        g_slots[...] += nn(oh_t, d_first)
        pl.when(i == 0)(node_ar.core_sum)
        pl.when(i == 2)(functools.partial(node_ar.axis_sum, 0))
        return carry

    lax.fori_loop(0, CHUNKS, backward, 0)

    put_small(small, 0, g_bias[...])
    put_small(small, 4, g_gain[...])
    put_flat(edge_flat, 0, g_in[...].astype(BF16))
    put_flat(edge_flat, 1536, g_out[...].astype(BF16))
    gs = g_slots[...].astype(BF16)
    put_flat(edge_flat, 512, (tn(x, gs[0:N, :]) + tn(table[...], gs[N:SLOTS, :])).astype(BF16))
    put_flat(edge_flat, 1024, tn(x, gs[SLOTS:, :]).astype(BF16))
    edge_ar.core_send()
    small_ar.core_send()

    slots[...] = nt(gs[N:SLOTS, :], ewi[D : 2 * D, :]).astype(BF16)
    for step in range(1, 8):
        peer = lax.rem(b + step, 8)
        send(
            slots.at[rows16(HALO + peer * 32, 32)], land_1b.at[rows16(b * 32, 32)], bs1, br1, (peer, t)
        )
    halo_swap(slots, halo_back, b, t, bhs, bhr)
    land_1b[rows16(b * 32, 32), :] = slots[rows16(HALO + b * 32, 32), :]

    @pl.when(b == 0)
    def _():
        halo_back[0:32, :] = jnp.zeros((32, D), BF16)

    @pl.when(b == 7)
    def _():
        halo_back[32:64, :] = jnp.zeros((32, D), BF16)

    def edge_grad(i):
        rows = slice(i * CHUNK, (i + 1) * CHUNK)
        cots[rows, :] = (nn(slope_s[rows, :], ewiT[...]) + cots[rows, :].astype(F32)).astype(BF16)
        pltpu.make_async_copy(block(cots, i), block(grad_edges_h, i), out_sems.at[1, i]).start()

    def edge_result(i):
        rows = slice(i * CHUNK, (i + 1) * CHUNK)
        message = first_s[rows, :] * (eg[...] * live_mask(i))
        edges[rows, :] = (edges[rows, :].astype(F32) + message).astype(BF16)
        pltpu.make_async_copy(block(edges, i), block(edge_out_h, i), out_sems.at[0, i]).start()

    node_ar.axis_sum(1)
    edge_ar.core_sum()
    small_ar.core_sum()
    node_ar.axis_sum(2)
    for i in range(CHUNKS):
        edge_grad(i)
    totals[...] += nt(gs[0:N, :], ewi[D : 2 * D, :]) + nt(gs[SLOTS:, :], ewi[2 * D :, :])
    wait_bytes(land_1b.at[pl.ds(0, 224)], br1)
    far_2b[...] = nn(swap_order(16, 8), land_1b[...]).astype(BF16)
    for step in range(1, 16):
        peer = lax.rem(t + step, 16)
        send(
            far_2b.at[rows16(peer * 16, 16)], land_2b.at[rows16(t * 16, 16)], bs2, br2, (b, peer)
        )
    land_2b[rows16(t * 16, 16), :] = far_2b[rows16(t * 16, 16), :]
    node_ar.back(2)
    edge_ar.axis_sum(0)
    small_ar.axis_sum(0)
    edge_result(0)
    edge_result(1)
    node_ar.back(1)
    edge_ar.axis_sum(1)
    small_ar.axis_sum(1)
    edge_result(2)
    edge_result(3)
    edge_ar.axis_sum(2)
    small_ar.axis_sum(2)
    halo_wait(slots, halo_back, b, bhs, bhr)
    wait_bytes(slots.at[pl.ds(0, 224)], bs1)
    wait_bytes(land_2b.at[pl.ds(0, 240)], br2)
    wait_bytes(far_2b.at[pl.ds(0, 240)], bs2)
    far_back = tn(order[...], land_2b[...]).astype(BF16)
    returned = tn(picks[...], jnp.concatenate([halo_back[...], far_back], axis=0))
    grad_nodes[...] = (totals[...] + returned).astype(BF16)
    node_ar.back(0)
    for stage in (2, 1, 0):
        edge_ar.back(stage)
    for i in range(CHUNKS):
        pltpu.make_async_copy(block(edges, i), block(edge_out_h, i), out_sems.at[0, i]).wait()
        pltpu.make_async_copy(block(cots, i), block(grad_edges_h, i), out_sems.at[1, i]).wait()
    node_ar.finish()
    edge_ar.finish()


def final_kernel(
    edge_sum, node_sum, small, node_out, edge_out, grad_nodes, grad_edges,
    node_out_h, edge_out_h, grad_nodes_h, grad_edges_h, ewi_h, eb, ewo_h, eg, nwi_h, nb, nwo_h, ng,
    wide, parts, small_s, rows_s, through, in_sems, move_sems, sems,
):
    targets = [(nwi_h, 0, node_sum, 0), (nwi_h, 512, node_sum, 512), (nwo_h, 0, node_sum, 1024)]
    targets += [(ewi_h, 0, edge_sum, 0), (ewi_h, 512, edge_sum, 512), (ewi_h, 1024, edge_sum, 1024)]
    targets += [(ewo_h, 0, edge_sum, 1536)]

    def fetch(j):
        _, _, source, first = targets[j]
        return pltpu.make_async_copy(source.at[:, pl.ds(first, 512), :], parts.at[j], in_sems.at[j])

    small_copy = pltpu.make_async_copy(small, small_s, in_sems.at[7])
    for j in range(len(targets)):
        fetch(j).start()
    small_copy.start()
    copies = []
    moves = [(node_out, node_out_h, 0, N), (grad_nodes, grad_nodes_h, 0, N)]
    for i in range(CHUNKS):
        moves += [(edge_out, edge_out_h, i * CHUNK, CHUNK), (grad_edges, grad_edges_h, i * CHUNK, CHUNK)]
    places = [sum(size for _, _, _, size in moves[:j]) for j in range(len(moves))]

    def move(j, inward):
        source, target, first, size = moves[j]
        near = through.at[pl.ds(places[j], size)]
        if inward:
            return pltpu.make_async_copy(source.at[pl.ds(first, size)], near, move_sems.at[0, j])
        return pltpu.make_async_copy(near, target.at[pl.ds(first, size)], move_sems.at[1, j])

    for j in range(len(moves)):
        move(j, True).start()
    for j in range(len(moves)):
        move(j, True).wait()
        move(j, False).start()
        copies.append(move(j, False))
    for j, (ref, out_first, _, _) in enumerate(targets):
        fetch(j).wait()
        for k in range(4):
            wide[512 * j : 512 * (j + 1), 128 * k : 128 * (k + 1)] = parts[j, k].astype(F32)
        copy = pltpu.make_async_copy(
            wide.at[pl.ds(512 * j, 512)], ref.at[pl.ds(out_first, 512)], sems.at[4 + j]
        )
        copy.start()
        copies.append(copy)
    small_copy.wait()
    for j, ref in enumerate((eb, eg, nb, ng)):
        for k in range(4):
            rows_s[j, :, 128 * k : 128 * (k + 1)] = small_s[4 * j + k : 4 * j + k + 1, :]
        copy = pltpu.make_async_copy(rows_s.at[j], ref, sems.at[11 + j])
        copy.start()
        copies.append(copy)
    for copy in copies:
        copy.wait()


def vmem(count):
    return [pl.BlockSpec(memory_space=pltpu.VMEM)] * count


def shape(rows, dtype=BF16, width=D):
    return jax.ShapeDtypeStruct((rows, width), dtype)


def reduce_scratch(total):
    v, half = pltpu.VMEM, total // 2
    return [
        v((half, 128), BF16),
        v((half, 128), BF16),
        v((half // 4 * 3, 128), BF16),
        v((half // 16 * 3, 128), BF16),
        v((half // 64 * 3, 128), BF16),
        v((half // 4, 128), BF16),
        v((half // 16, 128), BF16),
    ]


def step(*operands):
    dma = pltpu.SemaphoreType.DMA
    hbm = pl.BlockSpec(memory_space=pltpu.HBM)
    v = pltpu.VMEM
    wide = v((EDGES, D), BF16)
    square = v((D, D), BF16)
    total = v((D, D), F32)
    return pl.pallas_call(
        step_kernel,
        out_shape=(
            shape(N),
            shape(N),
            shape(4 * EDGE_ROWS, BF16, 128),
            shape(4 * NODE_ROWS, BF16, 128),
            shape(16, F32, 128),
            shape(EDGES),
            shape(EDGES),
        ),
        in_specs=[pl.BlockSpec(memory_space=pltpu.SMEM)] + [hbm] * 16,
        out_specs=tuple(vmem(5) + [hbm] * 2),
        scratch_shapes=[
            v((1, 4, 32), jnp.int32),
            v((1, 2, 128), jnp.int32),
            v((1, EDGES), jnp.int32),
            v((1, EDGES), jnp.int32),
            v((N, D), BF16),
            v((N, D), BF16),
            v((1, D), F32),
            v((1, D), F32),
            v((1, D), F32),
            v((1, D), F32),
            wide,
            wide,
            v((3 * D, D), BF16),
            square,
            v((2 * D, D), BF16),
            square,
            v((D + 2 * N, D), BF16),
            v((TABLE, D), BF16),
            square,
            square,
            v((EDGES, D), F32),
            wide,
            wide,
            v((EDGES, 1), F32),
            v((EDGES, N), BF16),
            v((TABLE, N), BF16),
            v((FAR, FAR), BF16),
            v((N, D), F32),
            total,
            total,
            v((SLOTS + N, D), F32),
            v((1, D), F32),
            v((1, D), F32),
            v((N, D), F32),
            v((TABLE, D), BF16),
            v((16, 128), F32),
            v((TABLE, D), BF16),
            v((TABLE, D), BF16),
            v((FAR, D), BF16),
            v((FAR, D), BF16),
            v((4 * EDGE_ROWS, 128), BF16),
            v((4 * NODE_ROWS, 128), BF16),
        ]
        + reduce_scratch(4 * EDGE_ROWS)
        + reduce_scratch(4 * NODE_ROWS)
        + [
            v((3, 16, 128), F32),
            v((13, 16, 128), F32),
            v((HALO, D), BF16),
            v((FAR, D), BF16),
            v((FAR, D), BF16),
            v((FAR, D), BF16),
            dma((10,)),
            dma((CHUNKS,)),
            dma((CHUNKS,)),
            dma((4,)),
            dma((2, CHUNKS)),
        ]
        + [dma((4,)), dma((4,)), dma(()), dma(()), dma(()), dma(())] * 2
        + [dma((4,)), dma((4,)), dma((8, 3)), dma((8, 3)), dma((8, 3)), dma((8, 3))],
        compiler_params=pltpu.CompilerParams(
            collective_id=0, has_side_effects=True, vmem_limit_bytes=VMEM_LIMIT
        ),
    )(*operands)


def final(edge_sum, node_sum, small, node_out, edge_out, grad_nodes, grad_edges):
    hbm = pl.BlockSpec(memory_space=pl.ANY)
    v, dma = pltpu.VMEM, pltpu.SemaphoreType.DMA
    return pl.pallas_call(
        final_kernel,
        out_shape=(
            shape(N), shape(EDGES), shape(N), shape(EDGES),
            shape(1536, F32), shape(1, F32), shape(512, F32), shape(1, F32),
            shape(1024, F32), shape(1, F32), shape(512, F32), shape(1, F32),
        ),
        in_specs=[hbm] * 7,
        out_specs=(hbm,) * 12,
        scratch_shapes=[
            v((3584, D), F32),
            v((7, 4, 512, 128), BF16),
            v((16, 128), F32),
            v((4, 1, D), F32),
            v((2 * N + 2 * EDGES, D), BF16),
            dma((8,)),
            dma((2, 2 + 2 * CHUNKS)),
            dma((15,)),
        ],
        compiler_params=pltpu.CompilerParams(vmem_limit_bytes=VMEM_LIMIT),
    )(edge_sum.reshape(4, EDGE_ROWS, 128), node_sum.reshape(4, NODE_ROWS, 128), small, node_out, edge_out, grad_nodes, grad_edges)


def shards(
    node_latents, edge_latents, edge_count, receiver, sender, halo_send, far_send,
    edge_weight_in, edge_bias, edge_weight_out, edge_gain,
    node_weight_in, node_bias, node_weight_out, node_gain, cot_nodes, cot_edges,
):
    node_out, grad_nodes, edge_sum, node_sum, small, edge_out, grad_edges = step(
        edge_count, halo_send, far_send.transpose(0, 2, 1), sender.reshape(1, EDGES), receiver.reshape(1, EDGES),
        node_latents, cot_nodes,
        edge_bias.reshape(1, D), edge_gain.reshape(1, D), node_bias.reshape(1, D), node_gain.reshape(1, D),
        edge_latents, cot_edges, edge_weight_in, edge_weight_out, node_weight_in, node_weight_out,
    )
    outs = final(edge_sum, node_sum, small, node_out, edge_out, grad_nodes, grad_edges)
    return tuple(out.reshape(D) if out.shape[0] == 1 else out for out in outs)


def solution(mesh):
    split = ("lat", "lon")
    rows, flat = P(split, None), P(split)
    cube, whole = P(split, None, None), P()
    return jax.shard_map(
        shards,
        mesh=mesh,
        in_specs=(rows, rows, flat, flat, flat, cube, cube) + (whole,) * 8 + (rows, rows),
        out_specs=(rows, rows, rows, rows) + (whole,) * 8,
        check_vma=False,
    )
```

time: 113 us -> 89.3 us (0.79)
  Pallas kernels: 102 us -> 87.7 us
  local copies, waits for them, and re-layouts: 9.3 us -> 0 us
    pallas_call x4 -> x2, Pallas kernels: 102 us -> 87.7 us  [the longest x1 79.8 us: step(): pl.pallas_call(step_kernel, out_shape=(shape(N), shape(N), shape(4 * EDGE...]
    unnamed x14 -> x0, local copies, waits for them, and re-layouts: 6.91 us -> none
    another operation x3 -> x0, local copies, waits for them, and re-layouts: 1.65 us -> none  [the longest x2 0.89 us: shards(): far = far_send[0].reshape(8, 16, 2).transpose(1, 0, 2).reshape(1, FAR)]
where the time goes in v2:
time: 89.3 us; the launch traced here: 89.2 us
  Pallas kernels  87.7 us (98%)
  between operations  1.46 us (2%)
    pallas_call x1, Pallas kernels, step(): pl.pallas_call(step_kernel, out_shape=(shape(N), shape(N), shape(4 * EDGE...  79.8 us
    pallas_call x1, Pallas kernels, final(): pl.pallas_call(final_kernel, out_shape=(shape(N), shape(EDGES), shape(N),...  7.88 us

profile of v2, /device:TPU:1, one launch (start us, length us, event | category | flops | bytes accessed | tf_op | source)
XLA Modules:
  0.0 89.2 jit_solution(3586614798988204337)
XLA Ops:
  1.3 79.8 %shard_map.256 = (bf16[256,512]{1,0:T(8,128)(2,1)}, bf16[256,512]{1,0:T(8,128)(2,1)}, bf16[8192,128]{1,0:T(8,128)(2,1)}, bf16[6144,128]{1,0:T(8,128)(2,1)}, f32[...) custom-call(s32[1]{0:T(128)S(6)} %copy.29.count, s32[1,4,32]{2,1,0:T(4,128)} %halo_send_h.1, ...), custom_call_target="tpu_custom_call" | custom-call | tf_op jit(solution)/shard_map/pallas_call | solution.py:693
  81.1 7.9 %shard_map.257 = (bf16[256,512]{1,0:T(8,128)(2,1)}, bf16[2048,512]{1,0:T(8,128)(2,1)}, bf16[256,512]{1,0:T(8,128)(2,1)}, bf16[2048,512]{1,0:T(8,128)(2,1)}, f32[...) custom-call(bf16[4,2048,128]{2,1,0:T(8,128)(2,1)} %bitcast.13, ...), custom_call_target="tpu_custom_call" | custom-call | tf_op jit(solution)/shard_map/pallas_call | solution.py:776

commit v3 on v2

--- a/solution.py
+++ b/solution.py
@@ -146,10 +146,11 @@
     return active, gate + active * (1.0 - gate)
 
 
-def put_flat(ref, first, values):
-    rows, total = values.shape[0], ref.shape[0] // 4
+def put_flat(ref, piece, values):
+    half = ref.shape[0] // 2
     for k in range(4):
-        ref[k * total + first : k * total + first + rows, :] = values[:, 128 * k : 128 * (k + 1)]
+        first = (k // 2) * half + piece * 1024 + (k % 2) * 512
+        ref[first : first + 512, :] = values[:, 128 * k : 128 * (k + 1)]
 
 
 def put_small(ref, first, values):
@@ -178,73 +179,103 @@
     def own(self, k, stage):
         return pick(self.axis(k, stage), self.xyz)
 
-    def mate(self, k, stage, step):
-        axis = self.axis(k, stage)
+    def mate(self, k, step):
+        axis = self.axis(k, 0)
         other = lax.rem(pick(axis, self.xyz) + step, 4)
         ox, oy, oz = (jnp.where(axis == a, other, v) for a, v in enumerate(self.xyz))
-        return other, (ox * 2 + self.core, oz * 4 + oy)
+        return ox * 2 + self.core, oz * 4 + oy
+
+    def plane_mate(self, k, step):
+        second, third = self.axis(k, 1), self.axis(k, 2)
+        c2 = lax.rem(pick(second, self.xyz) + step // 4, 4)
+        c3 = lax.rem(pick(third, self.xyz) + lax.rem(step, 4), 4)
+        ox, oy, oz = (
+            jnp.where(second == a, c2, jnp.where(third == a, c3, v)) for a, v in enumerate(self.xyz)
+        )
+        return c2 * 4 + c3, (ox * 2 + self.core, oz * 4 + oy)
 
 
 class AllReduce:
-    def __init__(self, place, parts, flat, result, half, land_c, lands, mids, gs, gr):
+    def __init__(self, place, parts, flat, result, half, land_c, land_a, land_p, mid, sems):
         self.at, self.parts, self.flat, self.result = place, parts, flat, result
-        self.half, self.land_c, self.lands = half, land_c, lands
-        self.sources = (half,) + mids
-        self.gs, self.gr = gs, gr
+        self.half, self.land_c, self.land_a, self.land_p, self.mid = half, land_c, land_a, land_p, mid
+        self.gs, self.gr, self.cr, self.ar = sems
         self.units = [sum(parts[:k]) for k in range(len(parts))]
         self.base = place.core * (flat.shape[0] // 2)
         self.other_base = (1 - place.core) * (flat.shape[0] // 2)
 
-    def core_send(self):
-        for k, s in enumerate(self.parts):
-            first = 64 * self.units[k]
+    def core_send(self, k):
+        size, first = 16 * self.parts[k], 64 * self.units[k]
+        own = pick(lax.rem((1 - self.at.core) + k, 3), self.at.xyz)
+        for step in (1, 2, 3, 0):
+            start = first + lax.rem(own + step, 4) * size
             send(
-                self.flat.at[rows16(self.other_base + first, 64 * s)],
-                self.land_c.at[rows16(first, 64 * s)],
+                self.flat.at[rows16(self.other_base + start, size)],
+                self.land_c.at[rows16(start, size)],
                 self.gs.at[0, k],
-                self.gr.at[0, k],
+                self.cr.at[k, step],
                 self.at.core_mate,
             )
 
-    def send_parts(self, k, stage):
-        size = (16, 4, 1)[stage] * self.parts[k]
-        first = (64, 16, 4)[stage] * self.units[k]
-        land_first = (16, 4, 1)[stage] * self.units[k] * 3
-        for step in range(1, 4):
-            other, device = self.at.mate(k, stage, step)
-            send(
-                self.sources[stage].at[rows16(first + other * size, size)],
-                self.lands[stage].at[rows16(land_first + (step - 1) * size, size)],
-                self.gs.at[1 + stage, k],
-                self.gr.at[1 + stage, k],
-                device,
-            )
-
     def core_sum(self):
+        for step in (1, 2, 3, 0):
+            for k, s in enumerate(self.parts):
+                size = 16 * s
+                start = 64 * self.units[k] + lax.rem(self.at.own(k, 0) + step, 4) * size
+                block = rows16(start, size)
+                wait_bytes(self.land_c.at[block], self.cr.at[k, step])
+                own = self.flat[rows16(self.base + start, size), :]
+                self.half[block, :] = (own.astype(F32) + self.land_c[block, :].astype(F32)).astype(BF16)
+                if step:
+                    send(
+                        self.half.at[block],
+                        self.land_a.at[rows16(48 * self.units[k] + (step - 1) * size, size)],
+                        self.gs.at[1, k],
+                        self.gr.at[1, k],
+                        self.at.mate(k, step),
+                    )
+
+    def axis_sum(self):
         for k, s in enumerate(self.parts):
-            mine = rows16(64 * self.units[k], 64 * s)
-            wait_bytes(self.land_c.at[mine], self.gr.at[0, k])
-            own = self.flat[rows16(self.base + 64 * self.units[k], 64 * s), :]
-            self.half[mine, :] = (own.astype(F32) + self.land_c[mine, :].astype(F32)).astype(BF16)
-            self.send_parts(k, 0)
-
-    def axis_sum(self, stage):
+            size, first, landed = 16 * s, 16 * self.units[k], 48 * self.units[k]
+            wait_bytes(self.land_a.at[rows16(landed, 3 * size)], self.gr.at[1, k])
+            own = rows16(64 * self.units[k] + self.at.own(k, 0) * size, size)
+            total = self.half[own, :].astype(F32)
+            for j in range(3):
+                total = total + self.land_a[rows16(landed + j * size, size), :].astype(F32)
+            self.mid[rows16(first, size), :] = total.astype(BF16)
+
+            def plane_send(step, carry, k=k, s=s, first=first):
+                block, device = self.at.plane_mate(k, step)
+                send(
+                    self.mid.at[rows16(first + block * s, s)],
+                    self.land_p.at[rows16(15 * self.units[k] + (step - 1) * s, s)],
+                    self.gs.at[2, k],
+                    self.gr.at[2, k],
+                    device,
+                )
+                return carry
+
+            lax.fori_loop(1, 16, plane_send, 0)
+
+    def plane_sum(self):
         for k, s in enumerate(self.parts):
-            size = (16, 4, 1)[stage] * s
-            first = (64, 16, 4)[stage] * self.units[k]
-            land_first = (16, 4, 1)[stage] * self.units[k] * 3
-            land = self.lands[stage]
-            wait_bytes(land.at[rows16(land_first, 3 * size)], self.gr.at[1 + stage, k])
-            total = self.sources[stage][rows16(first + self.at.own(k, stage) * size, size), :].astype(F32)
-            for j in range(3):
-                total = total + land[rows16(land_first + j * size, size), :].astype(F32)
-            total = total.astype(BF16)
-            if stage < 2:
-                self.sources[stage + 1][rows16((16, 4)[stage] * self.units[k], size), :] = total
-                self.send_parts(k, stage + 1)
-            else:
-                self.result[self.final(k, 3), :] = total
-                self.spread(k, 2)
+            landed = 15 * self.units[k]
+            wait_bytes(self.land_p.at[rows16(landed, 15 * s)], self.gr.at[2, k])
+            own = self.at.own(k, 1) * 4 + self.at.own(k, 2)
+            total = self.mid[rows16(16 * self.units[k] + own * s, s), :].astype(F32)
+            for j in range(15):
+                total = total + self.land_p[rows16(landed + j * s, s), :].astype(F32)
+            mine = self.final(k, 3)
+            self.result[mine, :] = total.astype(BF16)
+
+            def plane_spread(step, carry, k=k, mine=mine):
+                _, device = self.at.plane_mate(k, step)
+                block = self.result.at[mine]
+                send(block, block, self.gs.at[3, k], self.gr.at[3, k], device)
+                return carry
+
+            lax.fori_loop(1, 16, plane_spread, 0)
 
     def final(self, k, depth):
         start, size = self.base + 64 * self.units[k], 64 * self.parts[k]
@@ -253,31 +284,31 @@
             start = start + self.at.own(k, stage) * size
         return rows16(start, size)
 
-    def spread(self, k, stage):
-        block = self.result.at[self.final(k, stage + 1)]
-        for step in range(1, 4):
-            _, device = self.at.mate(k, stage, step)
-            send(block, block, self.gs.at[4 + stage, k], self.gr.at[4 + stage, k], device)
-
-    def back(self, stage):
+    def to_core(self, k, block):
+        send(block, block, self.gs.at[5, k], self.gr.at[5, k], self.at.core_mate)
+
+    def back_plane(self):
         for k, s in enumerate(self.parts):
-            size = (16, 4, 1)[stage] * s
-            wait_bytes(self.result.at[pl.ds(0, 3 * size)], self.gr.at[4 + stage, k])
-            if stage > 0:
-                self.spread(k, stage - 1)
-            else:
-                whole = self.result.at[self.final(k, 0)]
-                send(whole, whole, self.gs.at[7, k], self.gr.at[7, k], self.at.core_mate)
+            wait_bytes(self.result.at[pl.ds(0, 15 * s)], self.gr.at[3, k])
+            block = self.result.at[self.final(k, 1)]
+            for step in range(1, 4):
+                send(block, block, self.gs.at[4, k], self.ar.at[k, step - 1], self.at.mate(k, step))
+            self.to_core(k, block)
+
+    def back_axis(self):
+        for step in (1, 3, 2):
+            for k, s in enumerate(self.parts):
+                size = 16 * s
+                wait_bytes(self.result.at[pl.ds(0, size)], self.ar.at[k, step - 1])
+                other = lax.rem(self.at.own(k, 0) + (4 - step), 4)
+                start = self.base + 64 * self.units[k] + other * size
+                self.to_core(k, self.result.at[rows16(start, size)])
 
     def finish(self):
         for k, s in enumerate(self.parts):
-            wait_bytes(self.result.at[pl.ds(0, 64 * s)], self.gr.at[7, k])
-            wait_bytes(self.result.at[pl.ds(0, 64 * s)], self.gs.at[7, k])
-            wait_bytes(self.flat.at[pl.ds(0, 64 * s)], self.gs.at[0, k])
-            for stage in range(3):
-                size = (16, 4, 1)[stage] * s
-                wait_bytes(self.result.at[pl.ds(0, 3 * size)], self.gs.at[1 + stage, k])
-                wait_bytes(self.result.at[pl.ds(0, 3 * size)], self.gs.at[4 + stage, k])
+            wait_bytes(self.result.at[pl.ds(0, 64 * s)], self.gr.at[5, k])
+            for j, rows in enumerate((64, 48, 15, 15, 48, 64)):
+                wait_bytes(self.result.at[pl.ds(0, rows * s)], self.gs.at[j, k])
 
 
 class SmallSum:
@@ -329,11 +360,12 @@
     first_s, active_s, slope_s, scale_s, ohr_s,
     picks, order, gathered, g_in, g_out, g_slots, g_bias, g_gain, totals, slots, small,
     out_s, table, land_1, far_2, edge_flat, node_flat,
-    e_half, e_land_c, e_land_x, e_land_y, e_land_z, e_mid_x, e_mid_y,
-    n_half, n_land_c, n_land_x, n_land_y, n_land_z, n_mid_x, n_mid_y,
+    e_half, e_land_c, e_land_a, e_land_p, e_mid,
+    n_half, n_land_c, n_land_a, n_land_p, n_mid,
+    far_s, oht_s, node_pre,
     sm, sm_land, halo_back, land_1b, far_2b, land_2b,
     early_sems, in_sems, cot_sems, w_sems, out_sems,
-    hs, hr, s1, r1, s2, r2, bhs, bhr, bs1, br1, bs2, br2, ss, sr, egs, egr, ngs, ngr,
+    hs, hr, s1, r1, s2, r2, bhs, bhr, bs1, br1, bs2, br2, ss, sr, egs, egr, ecr, ear, ngs, ngr, ncr, nar,
 ):
     at = Place()
     b, t = at.b, at.t
@@ -423,7 +455,11 @@
     def local_part(i, carry):
         rows = rows_of(i)
         pltpu.make_async_copy(block(edges_h, i), block(edges, i), in_sems.at[i]).wait()
-        own = one_hot_rows(index_columns(sidx[:, rows]), 0, 2)
+        sent = index_columns(sidx[:, rows])
+        own = one_hot_rows(sent, 0, 2)
+        far_s[rows, :] = one_hot_rows(sent, N, 3)
+        oht_s[0:SLOTS, rows] = one_hot(iota((SLOTS, CHUNK), 0) == sidx[:, rows])
+        oht_s[SLOTS:, rows] = one_hot(iota((N, CHUNK), 0) == ridx[:, rows])
         ohr = one_hot_rows(index_columns(ridx[:, rows]), 0, 2)
         ohr_s[rows, :] = ohr
         first_s[rows, :] = nn(jnp.concatenate([edges[rows, :], own, ohr], axis=1), rhs[...]) + eb[...]
@@ -445,6 +481,9 @@
     lax.fori_loop(CHUNKS // 2, CHUNKS, local_part, 0)
     weight_copy(1).wait()
     ewoT[...] = ewo[...].T
+    weight_copy(2).wait()
+    weight_copy(3).wait()
+    node_pre[...] = nn(x, nwi[0:D, :]) + nb[...]
     halo_wait(out_s, table, b, hs, hr)
     wait_bytes(out_s.at[pl.ds(0, 240)], s1)
     wait_bytes(table.at[pl.ds(0, 224)], r2)
@@ -453,8 +492,7 @@
 
     def forward(i, carry):
         rows = rows_of(i)
-        far = one_hot_rows(index_columns(sidx[:, rows]), N, 3)
-        active, slope = silu_parts(first_s[rows, :] + nn(far, rhs_far[...]))
+        active, slope = silu_parts(first_s[rows, :] + nn(far_s[rows, :], rhs_far[...]))
         active = active.astype(BF16)
         active_s[rows, :] = active
         slope_s[rows, :] = slope.astype(BF16)
@@ -462,16 +500,13 @@
         first_s[rows, :] = hat
         scale_s[rows, :] = scale
         message = hat * eg[...] * live_mask(i)
-        ohr_t = one_hot(iota((N, CHUNK), 0) == ridx[:, rows])
-        gathered[...] += nn(ohr_t, message.astype(BF16))
+        gathered[...] += nn(oht_s[SLOTS:, rows], message.astype(BF16))
         return carry
 
     lax.fori_loop(0, CHUNKS, forward, 0)
 
-    weight_copy(2).wait()
-    weight_copy(3).wait()
     got = gathered[...].astype(BF16)
-    first = nn(x, nwi[0:D, :]) + nn(got, nwi[D:, :]) + nb[...]
+    first = node_pre[...] + nn(got, nwi[D:, :])
     active, slope = silu_parts(first)
     active = active.astype(BF16)
     hat, scale = norm_parts(nn(active, nwo[...]))
@@ -479,25 +514,26 @@
     cot = cot_nodes[...].astype(F32)
     put_small(small, 12, jnp.sum(cot * hat, axis=0, keepdims=True))
     d_second = norm_back(cot * ng[...], hat, scale).astype(BF16)
-    put_flat(node_flat, 1024, tn(active, d_second).astype(BF16))
+    put_flat(node_flat, 2, tn(active, d_second).astype(BF16))
     d_first = nt(d_second, nwo[...]) * slope
     put_small(small, 8, jnp.sum(d_first, axis=0, keepdims=True))
     d_first = d_first.astype(BF16)
     put_flat(node_flat, 0, tn(x, d_first).astype(BF16))
-    put_flat(node_flat, 512, tn(got, d_first).astype(BF16))
+    put_flat(node_flat, 1, tn(got, d_first).astype(BF16))
     totals[...] = nt(d_first, nwi[0:D, :]) + cot
     from_gathered = nt(d_first, nwi[D:, :]).astype(BF16)
 
     node_ar = AllReduce(
-        at, NODE_PARTS, node_flat, node_sum, n_half, n_land_c, (n_land_x, n_land_y, n_land_z),
-        (n_mid_x, n_mid_y), ngs, ngr,
+        at, NODE_PARTS, node_flat, node_sum, n_half, n_land_c, n_land_a, n_land_p, n_mid,
+        (ngs, ngr, ncr, nar),
     )
     edge_ar = AllReduce(
-        at, EDGE_PARTS, edge_flat, edge_sum, e_half, e_land_c, (e_land_x, e_land_y, e_land_z),
-        (e_mid_x, e_mid_y), egs, egr,
+        at, EDGE_PARTS, edge_flat, edge_sum, e_half, e_land_c, e_land_a, e_land_p, e_mid,
+        (egs, egr, ecr, ear),
     )
     small_ar = SmallSum(at, small, small_out, sm, sm_land, ss, sr)
-    node_ar.core_send()
+    for k in range(3):
+        node_ar.core_send(k)
 
     def backward(i, carry):
         rows = rows_of(i)
@@ -513,25 +549,23 @@
         d_first = d_first.astype(BF16)
         slope_s[rows, :] = d_first
         g_in[...] += tn(edges[rows, :], d_first)
-        oh_t = jnp.concatenate(
-            [one_hot(iota((SLOTS, CHUNK), 0) == sidx[:, rows]), one_hot(iota((N, CHUNK), 0) == ridx[:, rows])],
-            axis=0,
-        )
-        g_slots[...] += nn(oh_t, d_first)
+        g_slots[...] += nn(oht_s[:, rows], d_first)
         pl.when(i == 0)(node_ar.core_sum)
-        pl.when(i == 2)(functools.partial(node_ar.axis_sum, 0))
+        pl.when(i == 2)(node_ar.axis_sum)
         return carry
 
     lax.fori_loop(0, CHUNKS, backward, 0)
 
+    put_flat(edge_flat, 0, g_in[...].astype(BF16))
+    put_flat(edge_flat, 1, g_out[...].astype(BF16))
+    edge_ar.core_send(0)
+    gs = g_slots[...].astype(BF16)
+    put_flat(edge_flat, 2, (tn(x, gs[0:N, :]) + tn(table[...], gs[N:SLOTS, :])).astype(BF16))
+    edge_ar.core_send(1)
+    put_flat(edge_flat, 3, tn(x, gs[SLOTS:, :]).astype(BF16))
+    edge_ar.core_send(2)
     put_small(small, 0, g_bias[...])
     put_small(small, 4, g_gain[...])
-    put_flat(edge_flat, 0, g_in[...].astype(BF16))
-    put_flat(edge_flat, 1536, g_out[...].astype(BF16))
-    gs = g_slots[...].astype(BF16)
-    put_flat(edge_flat, 512, (tn(x, gs[0:N, :]) + tn(table[...], gs[N:SLOTS, :])).astype(BF16))
-    put_flat(edge_flat, 1024, tn(x, gs[SLOTS:, :]).astype(BF16))
-    edge_ar.core_send()
     small_ar.core_send()
 
     slots[...] = nt(gs[N:SLOTS, :], ewi[D : 2 * D, :]).astype(BF16)
@@ -562,10 +596,9 @@
         edges[rows, :] = (edges[rows, :].astype(F32) + message).astype(BF16)
         pltpu.make_async_copy(block(edges, i), block(edge_out_h, i), out_sems.at[0, i]).start()
 
-    node_ar.axis_sum(1)
+    node_ar.plane_sum()
     edge_ar.core_sum()
     small_ar.core_sum()
-    node_ar.axis_sum(2)
     for i in range(CHUNKS):
         edge_grad(i)
     totals[...] += nt(gs[0:N, :], ewi[D : 2 * D, :]) + nt(gs[SLOTS:, :], ewi[2 * D :, :])
@@ -577,18 +610,16 @@
             far_2b.at[rows16(peer * 16, 16)], land_2b.at[rows16(t * 16, 16)], bs2, br2, (b, peer)
         )
     land_2b[rows16(t * 16, 16), :] = far_2b[rows16(t * 16, 16), :]
-    node_ar.back(2)
-    edge_ar.axis_sum(0)
+    node_ar.back_plane()
+    edge_ar.axis_sum()
     small_ar.axis_sum(0)
     edge_result(0)
     edge_result(1)
-    node_ar.back(1)
-    edge_ar.axis_sum(1)
-    small_ar.axis_sum(1)
     edge_result(2)
     edge_result(3)
-    edge_ar.axis_sum(2)
-    small_ar.axis_sum(2)
+    node_ar.back_axis()
+    small_ar.axis_sum(1)
+    edge_ar.plane_sum()
     halo_wait(slots, halo_back, b, bhs, bhr)
     wait_bytes(slots.at[pl.ds(0, 224)], bs1)
     wait_bytes(land_2b.at[pl.ds(0, 240)], br2)
@@ -596,13 +627,13 @@
     far_back = tn(order[...], land_2b[...]).astype(BF16)
     returned = tn(picks[...], jnp.concatenate([halo_back[...], far_back], axis=0))
     grad_nodes[...] = (totals[...] + returned).astype(BF16)
-    node_ar.back(0)
-    for stage in (2, 1, 0):
-        edge_ar.back(stage)
+    small_ar.axis_sum(2)
+    edge_ar.back_plane()
     for i in range(CHUNKS):
         pltpu.make_async_copy(block(edges, i), block(edge_out_h, i), out_sems.at[0, i]).wait()
         pltpu.make_async_copy(block(cots, i), block(grad_edges_h, i), out_sems.at[1, i]).wait()
     node_ar.finish()
+    edge_ar.back_axis()
     edge_ar.finish()
 
 
@@ -611,13 +642,13 @@
     node_out_h, edge_out_h, grad_nodes_h, grad_edges_h, ewi_h, eb, ewo_h, eg, nwi_h, nb, nwo_h, ng,
     wide, parts, small_s, rows_s, through, in_sems, move_sems, sems,
 ):
-    targets = [(nwi_h, 0, node_sum, 0), (nwi_h, 512, node_sum, 512), (nwo_h, 0, node_sum, 1024)]
-    targets += [(ewi_h, 0, edge_sum, 0), (ewi_h, 512, edge_sum, 512), (ewi_h, 1024, edge_sum, 1024)]
-    targets += [(ewo_h, 0, edge_sum, 1536)]
+    targets = [(nwi_h, 0, node_sum, 0), (nwi_h, 512, node_sum, 1), (nwo_h, 0, node_sum, 2)]
+    targets += [(ewi_h, 0, edge_sum, 0), (ewi_h, 512, edge_sum, 2), (ewi_h, 1024, edge_sum, 3)]
+    targets += [(ewo_h, 0, edge_sum, 1)]
 
     def fetch(j):
-        _, _, source, first = targets[j]
-        return pltpu.make_async_copy(source.at[:, pl.ds(first, 512), :], parts.at[j], in_sems.at[j])
+        _, _, source, piece = targets[j]
+        return pltpu.make_async_copy(source.at[:, piece], parts.at[j], in_sems.at[j])
 
     small_copy = pltpu.make_async_copy(small, small_s, in_sems.at[7])
     for j in range(len(targets)):
@@ -645,7 +676,7 @@
     for j, (ref, out_first, _, _) in enumerate(targets):
         fetch(j).wait()
         for k in range(4):
-            wide[512 * j : 512 * (j + 1), 128 * k : 128 * (k + 1)] = parts[j, k].astype(F32)
+            wide[512 * j : 512 * (j + 1), 128 * k : 128 * (k + 1)] = parts[j, k // 2, k % 2].astype(F32)
         copy = pltpu.make_async_copy(
             wide.at[pl.ds(512 * j, 512)], ref.at[pl.ds(out_first, 512)], sems.at[4 + j]
         )
@@ -676,10 +707,8 @@
         v((half, 128), BF16),
         v((half, 128), BF16),
         v((half // 4 * 3, 128), BF16),
-        v((half // 16 * 3, 128), BF16),
-        v((half // 64 * 3, 128), BF16),
+        v((half // 64 * 15, 128), BF16),
         v((half // 4, 128), BF16),
-        v((half // 16, 128), BF16),
     ]
 
 
@@ -750,6 +779,9 @@
         + reduce_scratch(4 * EDGE_ROWS)
         + reduce_scratch(4 * NODE_ROWS)
         + [
+            v((EDGES, TABLE), BF16),
+            v((SLOTS + N, EDGES), BF16),
+            v((N, D), F32),
             v((3, 16, 128), F32),
             v((13, 16, 128), F32),
             v((HALO, D), BF16),
@@ -763,7 +795,8 @@
             dma((2, CHUNKS)),
         ]
         + [dma((4,)), dma((4,)), dma(()), dma(()), dma(()), dma(())] * 2
-        + [dma((4,)), dma((4,)), dma((8, 3)), dma((8, 3)), dma((8, 3)), dma((8, 3))],
+        + [dma((4,)), dma((4,))]
+        + [dma((6, 3)), dma((6, 3)), dma((3, 4)), dma((3, 3))] * 2,
         compiler_params=pltpu.CompilerParams(
             collective_id=0, has_side_effects=True, vmem_limit_bytes=VMEM_LIMIT
         ),
@@ -784,7 +817,7 @@
         out_specs=(hbm,) * 12,
         scratch_shapes=[
             v((3584, D), F32),
-            v((7, 4, 512, 128), BF16),
+            v((7, 2, 2, 512, 128), BF16),
             v((16, 128), F32),
             v((4, 1, D), F32),
             v((2 * N + 2 * EDGES, D), BF16),
@@ -793,7 +826,7 @@
             dma((15,)),
         ],
         compiler_params=pltpu.CompilerParams(vmem_limit_bytes=VMEM_LIMIT),
-    )(edge_sum.reshape(4, EDGE_ROWS, 128), node_sum.reshape(4, NODE_ROWS, 128), small, node_out, edge_out, grad_nodes, grad_edges)
+    )(edge_sum.reshape(2, 4, 2, 512, 128), node_sum.reshape(2, 3, 2, 512, 128), small, node_out, edge_out, grad_nodes, grad_edges)
 
 
 def shards(

time: 89.3 us -> 85.2 us (0.954)
  Pallas kernels: 87.7 us -> 83.6 us
    pallas_call x1, Pallas kernels: 79.8 us -> 75.7 us  [step(): pl.pallas_call(step_kernel, out_shape=(shape(N), shape(N), shape(4 * EDGE...]
where the time goes in v3:
time: 85.2 us; the launch traced here: 85 us
  Pallas kernels  83.6 us (98%)
  between operations  1.46 us (2%)
    pallas_call x1, Pallas kernels, step(): pl.pallas_call(step_kernel, out_shape=(shape(N), shape(N), shape(4 * EDGE...  75.7 us
    pallas_call x1, Pallas kernels, final(): pl.pallas_call(final_kernel, out_shape=(shape(N), shape(EDGES), shape(N),...  7.88 us

profile of v3, /device:TPU:1, one launch (start us, length us, event | category | flops | bytes accessed | tf_op | source)
XLA Modules:
  0.0 85.0 jit_solution(1431285930461373756)
XLA Ops:
  1.3 75.7 %shard_map.256 = (bf16[256,512]{1,0:T(8,128)(2,1)}, bf16[256,512]{1,0:T(8,128)(2,1)}, bf16[8192,128]{1,0:T(8,128)(2,1)}, bf16[6144,128]{1,0:T(8,128)(2,1)}, f32[...) custom-call(s32[1]{0:T(128)S(6)} %copy.29.count, s32[1,4,32]{2,1,0:T(4,128)} %halo_send_h.1, ...), custom_call_target="tpu_custom_call" | custom-call | tf_op jit(solution)/shard_map/pallas_call | solution.py:722
  77.0 7.9 %shard_map.257 = (bf16[256,512]{1,0:T(8,128)(2,1)}, bf16[2048,512]{1,0:T(8,128)(2,1)}, bf16[256,512]{1,0:T(8,128)(2,1)}, bf16[2048,512]{1,0:T(8,128)(2,1)}, f32[...) custom-call(bf16[2,4,2,512,128]{4,3,2,1,0:T(8,128)(2,1)} %bitcast.13, ...), custom_call_target="tpu_custom_call" | custom-call | tf_op jit(solution)/shard_map/pallas_call | solution.py:809

commit v4 on v3

--- a/solution.py
+++ b/solution.py
@@ -18,21 +18,17 @@
 FAR = 256
 TABLE = HALO + FAR
 SLOTS = N + TABLE
-CHUNK = 512
+CHUNK = 1024
 CHUNKS = EDGES // CHUNK
-EDGE_ROWS = 2048
-NODE_ROWS = 1536
-EDGE_PARTS = (32, 16, 16)
-NODE_PARTS = (16, 16, 16)
+EDGE_ROWS = 1536
+NODE_ROWS = 2048
+EDGE_PARTS = (16, 16, 16)
+NODE_PARTS = (32, 16, 16)
 VMEM_LIMIT = 63 * 1024 * 1024
 
 
 def nn(a, b):
     return jnp.dot(a, b, preferred_element_type=F32)
-
-
-def nt(a, b):
-    return lax.dot_general(a, b, (((1,), (1,)), ((), ())), preferred_element_type=F32)
 
 
 def tn(a, b):
@@ -126,11 +122,13 @@
     return one_hot(col == q * (2 * rows_major) + p * 2 + c)
 
 
-def norm_parts(values):
+def norm_parts(values, live=None):
     mean = jnp.mean(values, axis=-1, keepdims=True)
     centered = values - mean
     variance = jnp.mean(centered * centered, axis=-1, keepdims=True)
     scale = lax.rsqrt(variance + EPS)
+    if live is not None:
+        scale = scale * live
     return centered * scale, scale
 
 
@@ -304,9 +302,17 @@
                 start = self.base + 64 * self.units[k] + other * size
                 self.to_core(k, self.result.at[rows16(start, size)])
 
-    def finish(self):
+    def copy_out(self, target, sems, part):
+        half = self.flat.shape[0] // 2
+        rows = rows16((self.base, self.other_base)[part], half)
+        return pltpu.make_async_copy(self.result.at[rows], target.at[rows], sems.at[part])
+
+    def finish(self, target, sems):
+        self.copy_out(target, sems, 0).start()
         for k, s in enumerate(self.parts):
             wait_bytes(self.result.at[pl.ds(0, 64 * s)], self.gr.at[5, k])
+        self.copy_out(target, sems, 1).start()
+        for k, s in enumerate(self.parts):
             for j, rows in enumerate((64, 48, 15, 15, 48, 64)):
                 wait_bytes(self.result.at[pl.ds(0, rows * s)], self.gs.at[j, k])
 
@@ -354,17 +360,17 @@
 def step_kernel(
     count, halo_send_h, far_send_h, sidx_h, ridx_h, nodes_h, cot_nodes_h, eb_h, eg_h, nb_h, ng_h,
     edges_h, cot_edges_h, ewi_h, ewo_h, nwi_h, nwo_h,
-    node_out, grad_nodes, edge_sum, node_sum, small_out, edge_out_h, grad_edges_h,
+    node_out_h, grad_nodes_h, edge_sum_h, node_sum_h, small_out_h, edge_out_h, grad_edges_h,
     halo_send, far_send, sidx, ridx, nodes, cot_nodes, eb, eg, nb, ng,
-    edges, cots, ewi, ewo, nwi, nwo, rhs, rhs_far, ewoT, ewiT,
-    first_s, active_s, slope_s, scale_s, ohr_s,
+    edges, cots, ewi, ewo, nwi, nwo, rhs, rhs_far, ewoT, ewiT, nwoT, nwiT,
+    first_s, active_s, slope_s, hat_s, scale_s, ohr_s,
     picks, order, gathered, g_in, g_out, g_slots, g_bias, g_gain, totals, slots, small,
     out_s, table, land_1, far_2, edge_flat, node_flat,
     e_half, e_land_c, e_land_a, e_land_p, e_mid,
     n_half, n_land_c, n_land_a, n_land_p, n_mid,
-    far_s, oht_s, node_pre,
+    far_s, oht_s, node_pre, node_out, grad_nodes, edge_sum, node_sum, small_out,
     sm, sm_land, halo_back, land_1b, far_2b, land_2b,
-    early_sems, in_sems, cot_sems, w_sems, out_sems,
+    late_sems, early_sems, in_sems, cot_sems, w_sems, out_sems,
     hs, hr, s1, r1, s2, r2, bhs, bhr, bs1, br1, bs2, br2, ss, sr, egs, egr, ecr, ear, ngs, ngr, ncr, nar,
 ):
     at = Place()
@@ -443,7 +449,6 @@
     rhs[0:D, :] = ewi[0:D, :]
     rhs[D : D + N, :] = nn(x, ewi[D : 2 * D, :]).astype(BF16)
     rhs[D + N :, :] = nn(x, ewi[2 * D :, :]).astype(BF16)
-    ewiT[...] = ewi[0:D, :].T
     live = count[0]
 
     def rows_of(i):
@@ -483,6 +488,11 @@
     ewoT[...] = ewo[...].T
     weight_copy(2).wait()
     weight_copy(3).wait()
+    for k in range(2):
+        nwiT[:, D * k : D * (k + 1)] = nwi[D * k : D * (k + 1), :].T
+    nwoT[...] = nwo[...].T
+    for k in range(3):
+        ewiT[:, D * k : D * (k + 1)] = ewi[D * k : D * (k + 1), :].T
     node_pre[...] = nn(x, nwi[0:D, :]) + nb[...]
     halo_wait(out_s, table, b, hs, hr)
     wait_bytes(out_s.at[pl.ds(0, 240)], s1)
@@ -496,33 +506,35 @@
         active = active.astype(BF16)
         active_s[rows, :] = active
         slope_s[rows, :] = slope.astype(BF16)
-        hat, scale = norm_parts(nn(active, ewo[...]))
-        first_s[rows, :] = hat
+        hat, scale = norm_parts(nn(active, ewo[...]), live_mask(i))
+        hat = hat.astype(BF16)
+        hat_s[rows, :] = hat
         scale_s[rows, :] = scale
-        message = hat * eg[...] * live_mask(i)
-        gathered[...] += nn(oht_s[SLOTS:, rows], message.astype(BF16))
+        gathered[...] += nn(oht_s[SLOTS:, rows], hat)
         return carry
 
     lax.fori_loop(0, CHUNKS, forward, 0)
 
-    got = gathered[...].astype(BF16)
+    got = (gathered[...] * eg[...]).astype(BF16)
     first = node_pre[...] + nn(got, nwi[D:, :])
     active, slope = silu_parts(first)
     active = active.astype(BF16)
     hat, scale = norm_parts(nn(active, nwo[...]))
     node_out[...] = (x.astype(F32) + hat * ng[...]).astype(BF16)
+    node_out_copy = pltpu.make_async_copy(node_out, node_out_h, late_sems.at[4])
+    node_out_copy.start()
     cot = cot_nodes[...].astype(F32)
     put_small(small, 12, jnp.sum(cot * hat, axis=0, keepdims=True))
     d_second = norm_back(cot * ng[...], hat, scale).astype(BF16)
-    put_flat(node_flat, 2, tn(active, d_second).astype(BF16))
-    d_first = nt(d_second, nwo[...]) * slope
+    d_first = nn(d_second, nwoT[...]) * slope
     put_small(small, 8, jnp.sum(d_first, axis=0, keepdims=True))
     d_first = d_first.astype(BF16)
+    totals[...] = nn(d_first, nwiT[:, 0:D]) + cot
+    from_gathered = nn(d_first, nwiT[:, D:]).astype(BF16)
+
+    put_flat(node_flat, 2, tn(active, d_second).astype(BF16))
     put_flat(node_flat, 0, tn(x, d_first).astype(BF16))
     put_flat(node_flat, 1, tn(got, d_first).astype(BF16))
-    totals[...] = nt(d_first, nwi[0:D, :]) + cot
-    from_gathered = nt(d_first, nwi[D:, :]).astype(BF16)
-
     node_ar = AllReduce(
         at, NODE_PARTS, node_flat, node_sum, n_half, n_land_c, n_land_a, n_land_p, n_mid,
         (ngs, ngr, ncr, nar),
@@ -532,43 +544,50 @@
         (egs, egr, ecr, ear),
     )
     small_ar = SmallSum(at, small, small_out, sm, sm_land, ss, sr)
-    for k in range(3):
-        node_ar.core_send(k)
-
-    def backward(i, carry):
+    node_ar.core_send(0)
+    node_ar.core_send(1)
+
+    def backward_out(i, carry):
         rows = rows_of(i)
         pltpu.make_async_copy(block(cot_edges_h, i), block(cots, i), cot_sems.at[i]).wait()
         ce = cots[rows, :].astype(F32)
-        hat = first_s[rows, :]
-        d_message = (ce + nn(ohr_s[rows, :], from_gathered)) * live_mask(i)
+        hat = hat_s[rows, :].astype(F32)
+        d_message = ce + nn(ohr_s[rows, :], from_gathered)
         g_gain[...] += jnp.sum(d_message * hat, axis=0, keepdims=True)
         d_second = norm_back(d_message * eg[...], hat, scale_s[rows, :]).astype(BF16)
         g_out[...] += tn(active_s[rows, :], d_second)
-        d_first = nn(d_second, ewoT[...]) * slope_s[rows, :].astype(F32)
+        active_s[rows, :] = d_second
+        return carry
+
+    lax.fori_loop(0, CHUNKS, backward_out, 0)
+    put_flat(node_flat, 3, g_out[...].astype(BF16))
+    node_ar.core_send(2)
+
+    def backward_in(i, carry):
+        rows = rows_of(i)
+        d_first = nn(active_s[rows, :], ewoT[...]) * slope_s[rows, :].astype(F32)
         g_bias[...] += jnp.sum(d_first, axis=0, keepdims=True)
         d_first = d_first.astype(BF16)
         slope_s[rows, :] = d_first
         g_in[...] += tn(edges[rows, :], d_first)
         g_slots[...] += nn(oht_s[:, rows], d_first)
         pl.when(i == 0)(node_ar.core_sum)
-        pl.when(i == 2)(node_ar.axis_sum)
         return carry
 
-    lax.fori_loop(0, CHUNKS, backward, 0)
+    lax.fori_loop(0, CHUNKS, backward_in, 0)
 
     put_flat(edge_flat, 0, g_in[...].astype(BF16))
-    put_flat(edge_flat, 1, g_out[...].astype(BF16))
     edge_ar.core_send(0)
     gs = g_slots[...].astype(BF16)
-    put_flat(edge_flat, 2, (tn(x, gs[0:N, :]) + tn(table[...], gs[N:SLOTS, :])).astype(BF16))
+    put_flat(edge_flat, 1, (tn(x, gs[0:N, :]) + tn(table[...], gs[N:SLOTS, :])).astype(BF16))
     edge_ar.core_send(1)
-    put_flat(edge_flat, 3, tn(x, gs[SLOTS:, :]).astype(BF16))
+    put_flat(edge_flat, 2, tn(x, gs[SLOTS:, :]).astype(BF16))
     edge_ar.core_send(2)
     put_small(small, 0, g_bias[...])
     put_small(small, 4, g_gain[...])
     small_ar.core_send()
 
-    slots[...] = nt(gs[N:SLOTS, :], ewi[D : 2 * D, :]).astype(BF16)
+    slots[...] = nn(gs[N:SLOTS, :], ewiT[:, D : 2 * D]).astype(BF16)
     for step in range(1, 8):
         peer = lax.rem(b + step, 8)
         send(
@@ -587,21 +606,21 @@
 
     def edge_grad(i):
         rows = slice(i * CHUNK, (i + 1) * CHUNK)
-        cots[rows, :] = (nn(slope_s[rows, :], ewiT[...]) + cots[rows, :].astype(F32)).astype(BF16)
+        cots[rows, :] = (nn(slope_s[rows, :], ewiT[:, 0:D]) + cots[rows, :].astype(F32)).astype(BF16)
         pltpu.make_async_copy(block(cots, i), block(grad_edges_h, i), out_sems.at[1, i]).start()
 
     def edge_result(i):
         rows = slice(i * CHUNK, (i + 1) * CHUNK)
-        message = first_s[rows, :] * (eg[...] * live_mask(i))
+        message = hat_s[rows, :].astype(F32) * eg[...]
         edges[rows, :] = (edges[rows, :].astype(F32) + message).astype(BF16)
         pltpu.make_async_copy(block(edges, i), block(edge_out_h, i), out_sems.at[0, i]).start()
 
-    node_ar.plane_sum()
     edge_ar.core_sum()
     small_ar.core_sum()
+    node_ar.axis_sum()
     for i in range(CHUNKS):
         edge_grad(i)
-    totals[...] += nt(gs[0:N, :], ewi[D : 2 * D, :]) + nt(gs[SLOTS:, :], ewi[2 * D :, :])
+    totals[...] += nn(gs[0:N, :], ewiT[:, D : 2 * D]) + nn(gs[SLOTS:, :], ewiT[:, 2 * D :])
     wait_bytes(land_1b.at[pl.ds(0, 224)], br1)
     far_2b[...] = nn(swap_order(16, 8), land_1b[...]).astype(BF16)
     for step in range(1, 16):
@@ -610,16 +629,14 @@
             far_2b.at[rows16(peer * 16, 16)], land_2b.at[rows16(t * 16, 16)], bs2, br2, (b, peer)
         )
     land_2b[rows16(t * 16, 16), :] = far_2b[rows16(t * 16, 16), :]
-    node_ar.back_plane()
     edge_ar.axis_sum()
     small_ar.axis_sum(0)
-    edge_result(0)
-    edge_result(1)
-    edge_result(2)
-    edge_result(3)
-    node_ar.back_axis()
+    node_ar.plane_sum()
+    for i in range(CHUNKS):
+        edge_result(i)
     small_ar.axis_sum(1)
     edge_ar.plane_sum()
+    node_ar.back_plane()
     halo_wait(slots, halo_back, b, bhs, bhr)
     wait_bytes(slots.at[pl.ds(0, 224)], bs1)
     wait_bytes(land_2b.at[pl.ds(0, 240)], br2)
@@ -627,14 +644,26 @@
     far_back = tn(order[...], land_2b[...]).astype(BF16)
     returned = tn(picks[...], jnp.concatenate([halo_back[...], far_back], axis=0))
     grad_nodes[...] = (totals[...] + returned).astype(BF16)
+    grad_nodes_copy = pltpu.make_async_copy(grad_nodes, grad_nodes_h, late_sems.at[5])
+    grad_nodes_copy.start()
     small_ar.axis_sum(2)
+    small_copy = pltpu.make_async_copy(small_out, small_out_h, late_sems.at[6])
+    small_copy.start()
     edge_ar.back_plane()
     for i in range(CHUNKS):
         pltpu.make_async_copy(block(edges, i), block(edge_out_h, i), out_sems.at[0, i]).wait()
         pltpu.make_async_copy(block(cots, i), block(grad_edges_h, i), out_sems.at[1, i]).wait()
-    node_ar.finish()
+    node_out_copy.wait()
+    node_ar.back_axis()
+    node_late, edge_late = late_sems.at[pl.ds(0, 2)], late_sems.at[pl.ds(2, 2)]
+    node_ar.finish(node_sum_h, node_late)
     edge_ar.back_axis()
-    edge_ar.finish()
+    edge_ar.finish(edge_sum_h, edge_late)
+    grad_nodes_copy.wait()
+    small_copy.wait()
+    for part in range(2):
+        node_ar.copy_out(node_sum_h, node_late, part).wait()
+        edge_ar.copy_out(edge_sum_h, edge_late, part).wait()
 
 
 def final_kernel(
@@ -643,8 +672,8 @@
     wide, parts, small_s, rows_s, through, in_sems, move_sems, sems,
 ):
     targets = [(nwi_h, 0, node_sum, 0), (nwi_h, 512, node_sum, 1), (nwo_h, 0, node_sum, 2)]
-    targets += [(ewi_h, 0, edge_sum, 0), (ewi_h, 512, edge_sum, 2), (ewi_h, 1024, edge_sum, 3)]
-    targets += [(ewo_h, 0, edge_sum, 1)]
+    targets += [(ewo_h, 0, node_sum, 3)]
+    targets += [(ewi_h, 0, edge_sum, 0), (ewi_h, 512, edge_sum, 1), (ewi_h, 1024, edge_sum, 2)]
 
     def fetch(j):
         _, _, source, piece = targets[j]
@@ -731,7 +760,7 @@
             shape(EDGES),
         ),
         in_specs=[pl.BlockSpec(memory_space=pltpu.SMEM)] + [hbm] * 16,
-        out_specs=tuple(vmem(5) + [hbm] * 2),
+        out_specs=(hbm,) * 7,
         scratch_shapes=[
             v((1, 4, 32), jnp.int32),
             v((1, 2, 128), jnp.int32),
@@ -752,8 +781,11 @@
             v((D + 2 * N, D), BF16),
             v((TABLE, D), BF16),
             square,
+            v((D, 3 * D), BF16),
             square,
+            v((D, 2 * D), BF16),
             v((EDGES, D), F32),
+            wide,
             wide,
             wide,
             v((EDGES, 1), F32),
@@ -782,12 +814,18 @@
             v((EDGES, TABLE), BF16),
             v((SLOTS + N, EDGES), BF16),
             v((N, D), F32),
+            v((N, D), BF16),
+            v((N, D), BF16),
+            v((4 * EDGE_ROWS, 128), BF16),
+            v((4 * NODE_ROWS, 128), BF16),
+            v((16, 128), F32),
             v((3, 16, 128), F32),
             v((13, 16, 128), F32),
             v((HALO, D), BF16),
             v((FAR, D), BF16),
             v((FAR, D), BF16),
             v((FAR, D), BF16),
+            dma((7,)),
             dma((10,)),
             dma((CHUNKS,)),
             dma((CHUNKS,)),
@@ -826,7 +864,7 @@
             dma((15,)),
         ],
         compiler_params=pltpu.CompilerParams(vmem_limit_bytes=VMEM_LIMIT),
-    )(edge_sum.reshape(2, 4, 2, 512, 128), node_sum.reshape(2, 3, 2, 512, 128), small, node_out, edge_out, grad_nodes, grad_edges)
+    )(edge_sum.reshape(2, 3, 2, 512, 128), node_sum.reshape(2, 4, 2, 512, 128), small, node_out, edge_out, grad_nodes, grad_edges)
 
 
 def shards(

time: 85.2 us -> 78.4 us (0.920)
  Pallas kernels: 83.6 us -> 76.8 us
    pallas_call x1, Pallas kernels: 75.7 us -> 68.9 us  [step(): pl.pallas_call(step_kernel, out_shape=(shape(N), shape(N), shape(4 * EDGE...]
where the time goes in v4:
time: 78.4 us; the launch traced here: 78.3 us
  Pallas kernels  76.8 us (98%)
  between operations  1.48 us (2%)
    pallas_call x1, Pallas kernels, step(): pl.pallas_call(step_kernel, out_shape=(shape(N), shape(N), shape(4 * EDGE...  68.9 us
    pallas_call x1, Pallas kernels, final(): pl.pallas_call(final_kernel, out_shape=(shape(N), shape(EDGES), shape(N),...  7.89 us

profile of v4, /device:TPU:1, one launch (start us, length us, event | category | flops | bytes accessed | tf_op | source)
XLA Modules:
  0.0 78.3 jit_solution(16668539148336456482)
XLA Ops:
  1.3 68.9 %shard_map.256 = (bf16[256,512]{1,0:T(8,128)(2,1)}, bf16[256,512]{1,0:T(8,128)(2,1)}, bf16[6144,128]{1,0:T(8,128)(2,1)}, bf16[8192,128]{1,0:T(8,128)(2,1)}, f32[...) custom-call(s32[1]{0:T(128)S(6)} %copy.29.count, s32[1,4,32]{2,1,0:T(4,128)} %halo_send_h.1, ...), custom_call_target="tpu_custom_call" | custom-call | tf_op jit(solution)/shard_map/pallas_call | solution.py:751
  70.2 7.9 %shard_map.257 = (bf16[256,512]{1,0:T(8,128)(2,1)}, bf16[2048,512]{1,0:T(8,128)(2,1)}, bf16[256,512]{1,0:T(8,128)(2,1)}, bf16[2048,512]{1,0:T(8,128)(2,1)}, f32[...) custom-call(bf16[2,3,2,512,128]{4,3,2,1,0:T(8,128)(2,1)} %bitcast.14, ...), custom_call_target="tpu_custom_call" | custom-call | tf_op jit(solution)/shard_map/pallas_call | solution.py:847

commit v5 on v4

--- a/solution.py
+++ b/solution.py
@@ -364,7 +364,7 @@
     halo_send, far_send, sidx, ridx, nodes, cot_nodes, eb, eg, nb, ng,
     edges, cots, ewi, ewo, nwi, nwo, rhs, rhs_far, ewoT, ewiT, nwoT, nwiT,
     first_s, active_s, slope_s, hat_s, scale_s, ohr_s,
-    picks, order, gathered, g_in, g_out, g_slots, g_bias, g_gain, totals, slots, small,
+    picks, order, gathered, g_in, g_out, g_bias, g_gain, totals, slots, small,
     out_s, table, land_1, far_2, edge_flat, node_flat,
     e_half, e_land_c, e_land_a, e_land_p, e_mid,
     n_half, n_land_c, n_land_a, n_land_p, n_mid,
@@ -441,7 +441,6 @@
     gathered[...] = jnp.zeros_like(gathered)
     g_in[...] = jnp.zeros_like(g_in)
     g_out[...] = jnp.zeros_like(g_out)
-    g_slots[...] = jnp.zeros_like(g_slots)
     g_bias[...] = jnp.zeros_like(g_bias)
     g_gain[...] = jnp.zeros_like(g_gain)
 
@@ -570,7 +569,6 @@
         d_first = d_first.astype(BF16)
         slope_s[rows, :] = d_first
         g_in[...] += tn(edges[rows, :], d_first)
-        g_slots[...] += nn(oht_s[:, rows], d_first)
         pl.when(i == 0)(node_ar.core_sum)
         return carry
 
@@ -578,7 +576,7 @@
 
     put_flat(edge_flat, 0, g_in[...].astype(BF16))
     edge_ar.core_send(0)
-    gs = g_slots[...].astype(BF16)
+    gs = nn(oht_s[...], slope_s[...]).astype(BF16)
     put_flat(edge_flat, 1, (tn(x, gs[0:N, :]) + tn(table[...], gs[N:SLOTS, :])).astype(BF16))
     edge_ar.core_send(1)
     put_flat(edge_flat, 2, tn(x, gs[SLOTS:, :]).astype(BF16))
@@ -685,8 +683,7 @@
     small_copy.start()
     copies = []
     moves = [(node_out, node_out_h, 0, N), (grad_nodes, grad_nodes_h, 0, N)]
-    for i in range(CHUNKS):
-        moves += [(edge_out, edge_out_h, i * CHUNK, CHUNK), (grad_edges, grad_edges_h, i * CHUNK, CHUNK)]
+    moves += [(edge_out, edge_out_h, 0, EDGES), (grad_edges, grad_edges_h, 0, EDGES)]
     places = [sum(size for _, _, _, size in moves[:j]) for j in range(len(moves))]
 
     def move(j, inward):
@@ -795,7 +792,6 @@
             v((N, D), F32),
             total,
             total,
-            v((SLOTS + N, D), F32),
             v((1, D), F32),
             v((1, D), F32),
             v((N, D), F32),
@@ -860,7 +856,7 @@
             v((4, 1, D), F32),
             v((2 * N + 2 * EDGES, D), BF16),
             dma((8,)),
-            dma((2, 2 + 2 * CHUNKS)),
+            dma((2, 4)),
             dma((15,)),
         ],
         compiler_params=pltpu.CompilerParams(vmem_limit_bytes=VMEM_LIMIT),

time: 78.4 us -> 77.5 us (0.989)
  Pallas kernels: 76.8 us -> 75.9 us
where the time goes in v5:
time: 77.5 us; the launch traced here: 77.4 us
  Pallas kernels  75.9 us (98%)
  between operations  1.48 us (2%)
    pallas_call x1, Pallas kernels, step(): pl.pallas_call(step_kernel, out_shape=(shape(N), shape(N), shape(4 * EDGE...  68.4 us
    pallas_call x1, Pallas kernels, final(): pl.pallas_call(final_kernel, out_shape=(shape(N), shape(EDGES), shape(N),...  7.52 us

profile of v5, /device:TPU:1, one launch (start us, length us, event | category | flops | bytes accessed | tf_op | source)
XLA Modules:
  0.0 77.4 jit_solution(6776896763919109912)
XLA Ops:
  1.3 68.4 %shard_map.256 = (bf16[256,512]{1,0:T(8,128)(2,1)}, bf16[256,512]{1,0:T(8,128)(2,1)}, bf16[6144,128]{1,0:T(8,128)(2,1)}, bf16[8192,128]{1,0:T(8,128)(2,1)}, f32[...) custom-call(s32[1]{0:T(128)S(6)} %copy.29.count, s32[1,4,32]{2,1,0:T(4,128)} %halo_send_h.1, ...), custom_call_target="tpu_custom_call" | custom-call | tf_op jit(solution)/shard_map/pallas_call | solution.py:748
  69.7 7.5 %shard_map.257 = (bf16[256,512]{1,0:T(8,128)(2,1)}, bf16[2048,512]{1,0:T(8,128)(2,1)}, bf16[256,512]{1,0:T(8,128)(2,1)}, bf16[2048,512]{1,0:T(8,128)(2,1)}, f32[...) custom-call(bf16[2,3,2,512,128]{4,3,2,1,0:T(8,128)(2,1)} %bitcast.14, ...), custom_call_target="tpu_custom_call" | custom-call | tf_op jit(solution)/shard_map/pallas_call | solution.py:843

commit v6 on v5

--- a/solution.py
+++ b/solution.py
@@ -576,11 +576,12 @@
 
     put_flat(edge_flat, 0, g_in[...].astype(BF16))
     edge_ar.core_send(0)
-    gs = nn(oht_s[...], slope_s[...]).astype(BF16)
+    gr_sum = nn(oht_s[SLOTS:, :], slope_s[...]).astype(BF16)
+    put_flat(edge_flat, 2, tn(x, gr_sum).astype(BF16))
+    edge_ar.core_send(2)
+    gs = nn(oht_s[0:SLOTS, :], slope_s[...]).astype(BF16)
     put_flat(edge_flat, 1, (tn(x, gs[0:N, :]) + tn(table[...], gs[N:SLOTS, :])).astype(BF16))
     edge_ar.core_send(1)
-    put_flat(edge_flat, 2, tn(x, gs[SLOTS:, :]).astype(BF16))
-    edge_ar.core_send(2)
     put_small(small, 0, g_bias[...])
     put_small(small, 4, g_gain[...])
     small_ar.core_send()
@@ -618,7 +619,7 @@
     node_ar.axis_sum()
     for i in range(CHUNKS):
         edge_grad(i)
-    totals[...] += nn(gs[0:N, :], ewiT[:, D : 2 * D]) + nn(gs[SLOTS:, :], ewiT[:, 2 * D :])
+    totals[...] += nn(gs[0:N, :], ewiT[:, D : 2 * D]) + nn(gr_sum, ewiT[:, 2 * D :])
     wait_bytes(land_1b.at[pl.ds(0, 224)], br1)
     far_2b[...] = nn(swap_order(16, 8), land_1b[...]).astype(BF16)
     for step in range(1, 16):

time: 77.5 us -> 78.1 us (level)
  no operation moved by 1% of the time
where the time goes in v6:
time: 78.1 us; the launch traced here: 77.9 us
  Pallas kernels  76.5 us (98%)
  between operations  1.48 us (2%)
    pallas_call x1, Pallas kernels, step(): pl.pallas_call(step_kernel, out_shape=(shape(N), shape(N), shape(4 * EDGE...  68.9 us
    pallas_call x1, Pallas kernels, final(): pl.pallas_call(final_kernel, out_shape=(shape(N), shape(EDGES), shape(N),...  7.52 us

profile of v6, /device:TPU:1, one launch (start us, length us, event | category | flops | bytes accessed | tf_op | source)
XLA Modules:
  0.0 77.9 jit_solution(8623470605774509777)
XLA Ops:
  1.3 68.9 %shard_map.256 = (bf16[256,512]{1,0:T(8,128)(2,1)}, bf16[256,512]{1,0:T(8,128)(2,1)}, bf16[6144,128]{1,0:T(8,128)(2,1)}, bf16[8192,128]{1,0:T(8,128)(2,1)}, f32[...) custom-call(s32[1]{0:T(128)S(6)} %copy.29.count, s32[1,4,32]{2,1,0:T(4,128)} %halo_send_h.1, ...), custom_call_target="tpu_custom_call" | custom-call | tf_op jit(solution)/shard_map/pallas_call | solution.py:749
  70.2 7.5 %shard_map.257 = (bf16[256,512]{1,0:T(8,128)(2,1)}, bf16[2048,512]{1,0:T(8,128)(2,1)}, bf16[256,512]{1,0:T(8,128)(2,1)}, bf16[2048,512]{1,0:T(8,128)(2,1)}, f32[...) custom-call(bf16[2,3,2,512,128]{4,3,2,1,0:T(8,128)(2,1)} %bitcast.14, ...), custom_call_target="tpu_custom_call" | custom-call | tf_op jit(solution)/shard_map/pallas_call | solution.py:844
